TPU v7x, 128 devices: a whole 4x4x4 slice. The times are simulated.
128 devices in a mesh: ctx: 16 (over x_lo, y, core), ch: 8 (over z, x_hi).
Axes of the slice: x: 4 (x_hi: 2, x_lo: 2; x = x_hi * 2 + x_lo), y: 4, z: 4, core: 2. Of those that a mesh axis runs over, the one named last changes fastest.
Arguments:
- hidden: bfloat16 [8192, 4096], P('ctx', 'ch'), may hold values from -6 to 6
- norm_gain: float32 [2, 4096], replicated, may hold values from 0.5 to 2
- in_weight: bfloat16 [2, 4096, 3, 4096], P(None, 'ctx', None, 'ch'), may hold values from -0.09375 to 0.09375
- feat_filter: float32 [2, 3, 3, 4096], P(None, None, None, 'ch'), may hold values from -3 to 3
- se_filter: float32 [7, 4096], P(None, 'ch'), may hold values from -2 to 2
- mr_filter: float32 [128, 4096], P(None, 'ch'), may hold values from -0.5 to 0.5
- skip_gain: float32 [2, 4096], P(None, 'ch'), may hold values from -1 to 1
- out_weight: bfloat16 [2, 4096, 4096], P(None, 'ch', 'ctx'), may hold values from -0.125 to 0.125
Outputs:
- result: bfloat16 [8192, 4096], P('ctx', 'ch')
All inputs are finite; a program needn't handle non-finite values.
Results may differ from a plain program's by a relative error of at most 0.04.
Values may be sent and summed in bfloat16 or wider, within the bound.
No kernel may reach another device: no remote copies, remote signals or barrier semaphores. Data moves between devices by JAX's collectives and lax.ppermute only.
A program may use at most 128 MiB of HBM per device.

v0:
```python
import functools

import jax
import jax.numpy as jnp
import numpy as np
from jax import lax
from jax.experimental.layout import Layout, with_layout_constraint
from jax.experimental import pallas as pl
from jax.experimental.pallas import tpu as pltpu
from jax.sharding import Mesh, PartitionSpec as P

AXES = ("xl", "y", "core", "z", "xh")
HALF = 256
CUT = 1280
LANES = 128


def shift(value, axis, by):
    size = lax.axis_size(axis)
    return lax.ppermute(value, axis, [(i, (i + by) % size) for i in range(size)])


def swap(value):
    moved = lax.ppermute(value, ("core", "xh"), [(1, 2), (2, 1)])
    same = lax.axis_index("core") == lax.axis_index("xh")
    return jnp.where(same, value, moved)


def from_behind(value, axes):
    return lax.ppermute(value, axes, [(i, i + 1) for i in range(15)])


def by_rows(value):
    return with_layout_constraint(value, Layout(major_to_minor=tuple(range(value.ndim))))


def after(value, *others):
    return lax.optimization_barrier((value, *others))[0]


def together(*values):
    return lax.optimization_barrier(values)


def fetch(moves, sources, target, index_ref, semaphores):
    copies = []
    for number, (source, lead, lane, width, slot, other, by_rows, *fixed) in enumerate(moves):
        block = fixed[0] * 256 if slot is None else pl.multiple_of(index_ref[slot] * 256, 256)
        start = fixed[1] if len(fixed) > 1 else 0
        ref = sources[source]
        if lead is not None:
            ref = ref.at[lead]
        if by_rows:
            piece = target.at[pl.ds(pl.multiple_of(block + start, 128), ref.shape[0]), other : other + width]
        else:
            piece = target.at[other : other + ref.shape[0], pl.ds(block, 256)]
        copies.append(pltpu.make_async_copy(ref.at[:, lane : lane + width], piece, semaphores.at[number]))
    return copies


def norm_pieces(loads, places, raw, gain_ref, normed, squares):
    squares[...] = jnp.zeros_like(squares)
    for load, (j, start, count), place in zip(loads, pieces_of(len(loads)), places):
        load.wait()
        lanes = pl.ds(pl.multiple_of(place * 512, 512), 512)
        gain = gain_ref[pl.ds(place, 1), :]

        @pl.loop(0, count // 64)
        def _(step):
            rows = pl.ds(pl.multiple_of(start + step * 64, 64), 64)
            x = raw[j, rows, :].astype(jnp.float32)
            normed[rows, lanes] = (x * gain).astype(jnp.bfloat16)
            q = x * x
            squares[rows, :] += (q[:, :128] + q[:, 128:256]) + (q[:, 256:384] + q[:, 384:])

    squares[:, :1] = lax.rsqrt(jnp.sum(squares[...], axis=1, keepdims=True) * (1.0 / 4096) + 1e-06)


def pieces_of(count):
    rows = 8 * 2 * HALF // count
    return [(j % 8, j // 8 * rows, rows) for j in range(count)]


def in_kernel(moves, sources, halo, index_ref, place_ref, gain_ref, *refs):
    xs, refs = refs[:sources], refs[sources:]
    count = 1 + max(m[0] for m in moves)
    ws, refs = refs[:count], refs[count:]
    out_refs, (tail_ref, raw, normed, weights, squares, x_sems, w_sems) = refs[:2], refs[2:]
    xs = [xs[0].at[j // 2, j % 2] for j in range(8)] if sources == 1 else xs
    loads = [
        pltpu.make_async_copy(x, raw.at[j, start : start + rows], x_sems.at[number])
        for number, (x, (j, start, rows)) in enumerate(zip(xs, pieces_of(len(xs))))
    ]
    copies = fetch(moves, ws, weights, index_ref, w_sems)
    for copy in loads + copies:
        copy.start()
    norm_pieces(loads, [place_ref[j] for j in range(len(xs))], raw, gain_ref, normed, squares)
    for copy in copies:
        copy.wait()

    @pl.loop(0, 6)
    def _(step):
        lanes = pl.ds(pl.multiple_of(step * 256, 256), 256)
        product = jnp.dot(normed[...], weights[:, lanes], preferred_element_type=jnp.float32)
        product = (product * squares[:, :1]).astype(jnp.bfloat16)
        for part, out_ref in enumerate(out_refs):
            out_ref[:, lanes] = product[part * HALF : (part + 1) * HALF]

    last = out_refs[-1]
    tail_ref[:halo, :] = last[HALF - halo :, 512:]
    tail_ref[halo:, :512] = last[HALF - 16 :, :512]
    tail_ref[halo:, 512:] = jnp.zeros((16, 512), jnp.bfloat16)


def project_in(index, places, gain, pieces, weights, moves, halo):
    any_space = pl.BlockSpec(memory_space=pl.ANY)
    vmem = pl.BlockSpec(memory_space=pltpu.VMEM)
    smem = pl.BlockSpec(memory_space=pltpu.SMEM)
    return pl.pallas_call(
        functools.partial(in_kernel, moves, len(pieces), halo),
        out_shape=[jax.ShapeDtypeStruct((HALF, 1536), jnp.bfloat16)] * 2
        + [jax.ShapeDtypeStruct((halo + 16, 1024), jnp.bfloat16)],
        in_specs=[smem, smem, vmem] + [any_space] * (len(pieces) + len(weights)),
        out_specs=[vmem] * 3,
        scratch_shapes=[
            pltpu.VMEM((8, 2 * HALF, 512), jnp.bfloat16),
            pltpu.VMEM((2 * HALF, 4096), jnp.bfloat16),
            pltpu.VMEM((4096, 1536), jnp.bfloat16),
            pltpu.VMEM((2 * HALF, LANES), jnp.float32),
            pltpu.SemaphoreType.DMA((16,)),
            pltpu.SemaphoreType.DMA((len(moves),)),
        ],
        compiler_params=pltpu.CompilerParams(vmem_limit_bytes=50 * 1024 * 1024),
        cost_estimate=pl.CostEstimate(flops=4 * HALF * 4096 * 1536, bytes_accessed=18 * 2**20, transcendentals=0),
    )(index, places, gain, *pieces, *weights)


def filter_rows(halo, taps, before_ref, main_ref, feat_ref, filter_ref, skip_ref, inner, shaped, gated, copies8):
    total = halo + HALF

    if before_ref.shape[1] == 1024:
        shaped[:16, :512] = before_ref[halo:, :512].astype(jnp.float32)
        shaped[:halo, 512:] = before_ref[:halo, :].astype(jnp.float32)
    else:
        shaped[:16, :512] = before_ref[HALF - 16 :, :512].astype(jnp.float32)
        shaped[:halo, 512:] = before_ref[HALF - halo :, 512:].astype(jnp.float32)
    shaped[16 : 16 + HALF, :512] = main_ref[:, :512].astype(jnp.float32)
    shaped[halo:total, 512:] = main_ref[:, 512:].astype(jnp.float32)

    def feature(start, size, s, lanes):
        value = None
        for j in range(3):
            tap = feat_ref[3 * j + s : 3 * j + s + 1, lanes]
            low = s * 512 + lanes.start
            term = tap * shaped[start - j : start - j + size, low : low + LANES]
            value = term if value is None else value + term
        return value

    for lane in range(0, 512, LANES):
        lanes = slice(lane, lane + LANES)
        for start in range(8, total, 64):
            size = min(64, total - start)
            gated[start : start + size, lanes] = feature(start, size, 1, lanes) * feature(start, size, 2, lanes)
        gated[:8, lanes] = jnp.zeros((8, LANES), jnp.float32)

    if taps == 7:
        for lane in range(0, 512, LANES):
            lanes = slice(lane, lane + LANES)
            for start in range(0, HALF, 64):
                own = gated[halo + start : halo + start + 64, lanes]
                value = (skip_ref[:1, lanes] + filter_ref[:1, lanes]) * own
                for j in range(1, taps):
                    value = value + filter_ref[j : j + 1, lanes] * gated[halo + start - j : halo + start - j + 64, lanes]
                inner[start : start + 64, lanes] = (feature(16 + start, 64, 0, lanes) * value).astype(jnp.bfloat16)
    else:
        for lane in range(0, 512, LANES):
            lanes = slice(lane, lane + LANES)
            for r in range(8):
                for start in range(0, HALF + 128, 128):
                    copies8[r, start : start + 128, :] = gated[16 + start - r : 16 + start - r + 128, lanes]

            @pl.loop(0, HALF // 128)
            def _(step):
                base = pl.multiple_of(step * 128, 128)
                value = jnp.zeros((128, LANES), jnp.float32)
                for r in range(8):
                    for a in range(0, 16, 4):
                        window = copies8[r, pl.ds(pl.multiple_of(base + 128 - 8 * (a + 3), 8), 128 + 24), :]
                        for b in range(4):
                            tap = filter_ref[8 * (a + b) + r : 8 * (a + b) + r + 1, lanes]
                            low = 8 * (3 - b)
                            value = value + tap * window[low : low + 128]
                copies8[8, pl.ds(base, 128), :] = value

            for start in range(0, HALF, 64):
                own = gated[halo + start : halo + start + 64, lanes]
                value = copies8[8, start : start + 64, :] + skip_ref[:1, lanes] * own
                inner[start : start + 64, lanes] = (feature(16 + start, 64, 0, lanes) * value).astype(jnp.bfloat16)


def product_rows(outs, index_ref, inner, weights, out_refs):
    z = index_ref[0]
    core = index_ref[1]
    for by in range(4):
        block = lax.rem(z + by, 4)
        if outs == 4:
            columns = pl.ds(pl.multiple_of(block * 1024, 1024), 1024)
            out_refs[by][...] = jnp.dot(
                inner[...], weights[:, columns], preferred_element_type=jnp.float32
            ).astype(jnp.bfloat16)
        else:
            for side in range(2):
                place = block * 2 + (core if side == 0 else 1 - core)
                columns = pl.ds(pl.multiple_of(place * 512, 512), 512)
                out_refs[side][by] = jnp.dot(
                    inner[...], weights[:, columns], preferred_element_type=jnp.float32
                ).astype(jnp.bfloat16)


def filter_scratch(halo, taps):
    return [
        pltpu.VMEM((halo + HALF + 16, 1536), jnp.float32),
        pltpu.VMEM((halo + HALF, 512), jnp.float32),
        pltpu.VMEM((9, 8, LANES) if taps == 7 else (9, HALF + 128, LANES), jnp.float32),
    ]


def mix_kernel(moves, halo, taps, outs, index_ref, before_ref, main_ref, feat_ref, filter_ref, skip_ref, *refs):
    count = 1 + max(m[0] for m in moves)
    ws, refs = refs[:count], refs[count:]
    out_refs, refs = refs[:outs], refs[outs:]
    shaped, gated, copies8, inner, weights, w_sems = refs
    copies = fetch(moves, ws, weights, index_ref, w_sems)
    for copy in copies:
        copy.start()
    filter_rows(halo, taps, before_ref, main_ref, feat_ref, filter_ref, skip_ref, inner, shaped, gated, copies8)
    for copy in copies:
        copy.wait()
    product_rows(outs, index_ref, inner, weights, out_refs)


def mix_out(index, before, main, feat, taps, skip, weights, moves, halo, out_shapes):
    any_space = pl.BlockSpec(memory_space=pl.ANY)
    vmem = pl.BlockSpec(memory_space=pltpu.VMEM)
    length = taps.shape[0]
    return pl.pallas_call(
        functools.partial(mix_kernel, moves, halo, length, len(out_shapes)),
        out_shape=[jax.ShapeDtypeStruct(s, jnp.bfloat16) for s in out_shapes],
        in_specs=[pl.BlockSpec(memory_space=pltpu.SMEM)] + [vmem] * 5 + [any_space] * len(weights),
        out_specs=[vmem] * len(out_shapes),
        scratch_shapes=filter_scratch(halo, length)
        + [
            pltpu.VMEM((HALF, 512), jnp.bfloat16),
            pltpu.VMEM((512, 4096), jnp.bfloat16),
            pltpu.SemaphoreType.DMA((len(moves),)),
        ],
        compiler_params=pltpu.CompilerParams(vmem_limit_bytes=48 * 1024 * 1024),
        cost_estimate=pl.CostEstimate(flops=2 * HALF * 512 * 4096, bytes_accessed=6 * 2**20, transcendentals=0),
    )(index, before, main, feat, taps, skip, *weights)


def filter_kernel(halo, taps, before_ref, main_ref, feat_ref, filter_ref, skip_ref, inner, shaped, gated, copies8):
    filter_rows(halo, taps, before_ref, main_ref, feat_ref, filter_ref, skip_ref, inner, shaped, gated, copies8)


def filtered(before, main, feat, taps, skip, halo):
    vmem = pl.BlockSpec(memory_space=pltpu.VMEM)
    length = taps.shape[0]
    return pl.pallas_call(
        functools.partial(filter_kernel, halo, length),
        out_shape=jax.ShapeDtypeStruct((HALF, 512), jnp.bfloat16),
        in_specs=[vmem] * 5,
        out_specs=vmem,
        scratch_shapes=filter_scratch(halo, length),
        compiler_params=pltpu.CompilerParams(vmem_limit_bytes=24 * 1024 * 1024),
        cost_estimate=pl.CostEstimate(flops=2 * HALF * 512 * 4096 * 3, bytes_accessed=3 * 2**20, transcendentals=0),
    )(before, main, feat, taps, skip)


def product_kernel(moves, outs, index_ref, inner, weight_ref, *refs):
    out_refs, (weights, w_sems) = refs[:outs], refs[outs:]
    copies = fetch(moves, [weight_ref], weights, index_ref, w_sems)
    for copy in copies:
        copy.start()
    for copy in copies:
        copy.wait()
    product_rows(outs, index_ref, inner, weights, out_refs)


def project_out(index, inner, weight, moves, out_shapes):
    vmem = pl.BlockSpec(memory_space=pltpu.VMEM)
    return pl.pallas_call(
        functools.partial(product_kernel, moves, len(out_shapes)),
        out_shape=[jax.ShapeDtypeStruct(s, jnp.bfloat16) for s in out_shapes],
        in_specs=[pl.BlockSpec(memory_space=pltpu.SMEM), vmem, pl.BlockSpec(memory_space=pl.ANY)],
        out_specs=[vmem] * len(out_shapes),
        scratch_shapes=[pltpu.VMEM((512, 4096), jnp.bfloat16), pltpu.SemaphoreType.DMA((len(moves),))],
        compiler_params=pltpu.CompilerParams(vmem_limit_bytes=48 * 1024 * 1024),
        cost_estimate=pl.CostEstimate(flops=2 * HALF * 512 * 4096, bytes_accessed=6 * 2**20, transcendentals=0),
    )(index, inner, weight)


def per_device(hidden, norm_gain, in_weight, feat_filter, se_filter, mr_filter, skip_gain, out_weight):
    xl, y, core, z, xh = (lax.axis_index(a) for a in AXES)
    behind = lambda place, by: (place - by) % 4
    gains = norm_gain.reshape(2, 8, 512)
    ways = (1, -1, 2)
    other_core = lambda value: shift(value, "core", 1)
    gather = lambda value, axes: by_rows(lax.all_gather(by_rows(value), axes, axis=0, tiled=False))

    side_by_side = lambda w, o: jnp.concatenate([w.reshape(256, 1536), o[:256], o[256:]], axis=1)

    m = side_by_side(in_weight[0], out_weight[0])
    hidden_x, m_xl, m_up, m_down, w1 = together(
        shift(hidden, "xh", 1), shift(m, "xl", 1), shift(m, "y", 1), shift(m, "y", -1), swap(in_weight[1])
    )
    whole = by_rows(lax.all_gather(by_rows(jnp.stack([hidden, hidden_x])), "z", axis=0, tiled=False))
    most = m_xl[:, :CUT]
    far_top, far_low, most_up, most_down, rest = together(
        shift(m_up[:128], "y", 1),
        shift(m_down[128:], "y", -1),
        shift(most, "y", 1),
        shift(most, "y", -1),
        shift(jnp.stack([m_up[:, CUT:], m_down[:, CUT:]]), "xl", 1),
    )
    early = [m, m_xl, m_up, m_down, far_top, far_low, most_up, most_down, rest]
    most_top, most_low, rest_far, *early_other = together(
        shift(most_up[:128], "y", 1),
        shift(most_down[128:], "y", -1),
        shift(jnp.stack([far_top[:, CUT:], far_low[:, CUT:]]), "xl", 1),
        *[other_core(v) for v in early],
    )
    late = [most_top, most_low, rest_far]
    w_list = early + early_other + late + [other_core(v) for v in late]
    w_moves, q_moves, slots = [], [], [z, core]

    def take(number, lead, at_xl, at_y, at_core, low, high, start):
        w_moves.append((number, lead, 0, min(high, 1536) - low, len(slots), low, True, None, start))
        if high == 2048:
            for half in range(2):
                q_moves.append((number, lead, 1536 + 256 * half - low, 256, len(slots), 256 * half + start, False))
        slots.append(at_xl * 8 + at_y * 2 + at_core)

    up, down, far = behind(y, 1), behind(y, -1), behind(y, 2)
    for number, last, c in ((0, 18, core), (9, 21, 1 - core)):
        take(number, None, xl, y, c, 0, 2048, 0)
        take(number + 1, None, 1 - xl, y, c, 0, 2048, 0)
        take(number + 2, None, xl, up, c, 0, 2048, 0)
        take(number + 3, None, xl, down, c, 0, 2048, 0)
        take(number + 4, None, xl, far, c, 0, 2048, 0)
        take(number + 5, None, xl, far, c, 0, 2048, 128)
        take(number + 6, None, 1 - xl, up, c, 0, CUT, 0)
        take(number + 7, None, 1 - xl, down, c, 0, CUT, 0)
        take(number + 8, 0, 1 - xl, up, c, CUT, 2048, 0)
        take(number + 8, 1, 1 - xl, down, c, CUT, 2048, 0)
        take(last, None, 1 - xl, far, c, 0, CUT, 0)
        take(last + 1, None, 1 - xl, far, c, 0, CUT, 128)
        take(last + 2, 0, 1 - xl, far, c, CUT, 2048, 0)
        take(last + 2, 1, 1 - xl, far, c, CUT, 2048, 128)
    q_index = jnp.stack(slots).astype(jnp.int32)
    q_list = w_list

    w1 = gather(after(w1.reshape(256, 1536), rest), ("xh", "xl", "y"))
    o1 = gather(swap(after(out_weight[1], rest_far)), ("xh", "xl", "y"))
    small = jnp.concatenate([feat_filter[1].reshape(9, 512), skip_gain[1:2], mr_filter], axis=0)

    places = jnp.stack([2 * p + c for p in range(4) for c in (xh, 1 - xh)]).astype(jnp.int32)
    low, high, tail = project_in(q_index, places, gains[0], [whole], w_list, w_moves, 16)
    base, small = after((hidden, small), low)
    base, small = swap(base), swap(small)
    tail = from_behind(tail, ("xl", "y", "core"))

    def first_parts(before, main):
        parts = mix_out(
            q_index, before, main, feat_filter[0].reshape(9, 512), se_filter, skip_gain[0:1], q_list, q_moves, 16,
            [(HALF, 1024)] * 4,
        )
        return parts[0], [shift(part, "z", by) for by, part in ((1, parts[1]), (-1, parts[3]), (2, parts[2]))]

    def over_z(own, received):
        total = own.astype(jnp.float32)
        for value in received:
            total = total + value.astype(jnp.float32)
        total = total.astype(jnp.bfloat16)
        pick = lambda c: jnp.where(c == 0, total[:, :512], total[:, 512:])
        mine, others = pick(core), pick(1 - core)
        return mine, [
            lax.ppermute(mine, ("core", "xh"), [(1, 0), (2, 3)]),
            lax.ppermute(others, ("core", "xh"), [(1, 2), (2, 1)]),
            lax.ppermute(others, ("core", "xh"), [(0, 2), (3, 1)]),
        ]

    def over_x(mine, received, rows):
        kept = jnp.where(core == xh, mine, jnp.zeros_like(mine))
        current = base[rows : rows + HALF].astype(jnp.float32) + kept.astype(jnp.float32)
        for value in received:
            current = current + value.astype(jnp.float32)
        return current.astype(jnp.bfloat16)

    own_high, high_z = first_parts(low, high)
    own_low, low_z = first_parts(tail, low)
    mine_high, high_x = over_z(own_high, high_z)
    *low_z, one, two, three = together(*low_z, *high_x)
    high = over_x(mine_high, (one, two, three), HALF)
    mine_low, low_x = over_z(own_low, low_z)
    high = after(high, low_x[2])
    high_near = [shift(high, "z", by) for by in ways]
    one, two, three, *high_near = together(*low_x, *high_near)
    low = over_x(mine_low, (one, two, three), 0)

    places = [(p, (p // 4 % 2) * 8 + (p % 4) * 2 + p // 8) for p in range(16)]
    w_moves = [(0, p, 0, 1536, None, 0, True, block) for p, block in places]
    p_moves = [(0, p, 0, 256, None, 0, False, block) for p, block in places]
    x_index = jnp.stack([behind(z, by) * 2 + c for c in (core, 1 - core) for by in (0, *ways)] * 2).astype(jnp.int32)
    low_near = [low] + [shift(low, "z", by) for by in ways]
    high_near = [high] + high_near
    high_far = [other_core(v) for v in high_near]
    low_far = [other_core(v) for v in low_near]
    p_low, p_high, tail = project_in(
        q_index, x_index, gains[1], low_near + low_far + high_near + high_far, [w1], w_moves, 144
    )
    tail = from_behind(tail, ("xl", "y", "xh"))

    def second_filter(before, main):
        return filtered(before, main, small[:9], small[10:], small[9:10], 144)

    def second_parts(inner):
        return project_out(q_index, inner, o1, p_moves, [(4, HALF, 512)] * 2)

    def second_z(own, theirs):
        both = (own.astype(jnp.float32) + theirs.astype(jnp.float32)).astype(jnp.bfloat16)
        return both[0], [shift(both[at], "z", by) for by, at in ((1, 1), (-1, 3), (2, 2))]

    def second_sum(own, received, rows):
        total = rows.astype(jnp.float32) + own.astype(jnp.float32)
        for value in received:
            total = total + value.astype(jnp.float32)
        return swap(total.astype(jnp.bfloat16))

    inner_high = second_filter(p_low, p_high)
    inner_low = second_filter(tail, p_low)
    inner_high, inner_low = together(inner_high, inner_low)
    own_high, theirs_high = second_parts(inner_high)
    theirs_high = other_core(theirs_high)
    own_high, high_z = second_z(own_high, theirs_high)
    own_low, theirs_low = second_parts(inner_low)
    theirs_low = other_core(theirs_low)
    high = second_sum(own_high, high_z, high)
    own_low, low_z = second_z(own_low, theirs_low)
    low = second_sum(own_low, low_z, low)
    return jnp.concatenate([low, high], axis=0)


def solution(mesh):
    fine = Mesh(np.asarray(mesh.devices).reshape(2, 4, 2, 4, 2), AXES)
    ctx, ch = ("xl", "y", "core"), ("z", "xh")
    return jax.shard_map(
        per_device,
        mesh=fine,
        in_specs=(
            P(ctx, ch),
            P(),
            P(None, ctx, None, ch),
            P(None, None, None, ch),
            P(None, ch),
            P(None, ch),
            P(None, ch),
            P(None, ch, ctx),
        ),
        out_specs=P(ctx, ch),
        check_vma=False,
    )
```

profile of v0, /device:TPU:25, one launch (start us, length us, event | category | flops | bytes accessed | tf_op | source)
XLA Modules:
  0.0 340.6 jit_solution(18008947699936169303)
XLA Ops:
  8.3 5.2 %collective-permute-start.4 = (bf16[256,3,512]{0,2,1:T(8,128)(2,1)S(1)}, bf16[256,3,512]{0,2,1:T(8,128)(2,1)}, u32[]{:S(2)}, u32[]{:S(2)}) collective-permute-start(bf16[256,3,512]{0,2,1:T(8,128)(2,1)S(1)} %bitcast.82), channel_id=1, source_target_pairs={{1,8},{8,1},{3,10},{10,3},{5,12},{12,5},{7,14},{14,7},{17,24},{24,... | collective-permute-start | bytes 2359304 | tf_op jit(solution)/shard_map/ppermute | solution.py:24
  16.2 15.1 %collective-permute-done.4 = bf16[256,3,512]{0,2,1:T(8,128)(2,1)} collective-permute-done((bf16[256,3,512]{0,2,1:T(8,128)(2,1)S(1)}, bf16[256,3,512]{0,2,1:T(8,128)(2,1)}, u32[]{:S(2)}, u32[]{:S(2)}) %collective-permute-start.4) | collective-permute-done | bytes 786464 | tf_op jit(solution)/shard_map/ppermute | solution.py:24
  31.3 2.1 broadcast_select_fusion
  33.4 22.3 %collective-permute-done = bf16[512,512]{1,0:T(8,128)(2,1)S(1)} collective-permute-done((bf16[512,512]{1,0:T(8,128)(2,1)S(1)}, bf16[512,512]{1,0:T(8,128)(2,1)S(1)}, u32[]{:S(2)}, u32[]{:S(2)}) %collective-permute-start) | collective-permute-done | bytes 524320 | tf_op jit(solution)/shard_map/ppermute | solution.py:20
  64.8 20.0 %collective-permute-done.5.refs_5_.refs_4_ = bf16[128,2048]{1,0:T(8,128)(2,1)S(1)} collective-permute-done((bf16[128,2048]{1,0:T(8,128)(2,1)S(1)}, bf16[128,2048]{1,0:T(8,128)(2,1)S(1)}, u32[]{:S(2)}, u32[]{:S(2)}) %collective-permute-start.5) | collective-permute-done | bytes 524320 | tf_op jit(solution)/shard_map/ppermute | solution.py:20
  86.0 2.6 copy.18
  88.6 3.5 %collective-permute-start.13 = (bf16[256,2048]{1,0:T(8,128)(2,1)S(1)}, bf16[256,2048]{1,0:T(8,128)(2,1)S(1)}, u32[]{:S(2)}, u32[]{:S(2)}) collective-permute-start(bf16[256,2048]{1,0:T(8,128)(2,1)S(1)} %pad_maximum_fusion.refs_1_.refs_0_), channel_id=1, source_target_pairs={{0,8},{8,0},{1,9},{9,1},{2,10},{10,2},{3,11},{11,3},{4,12},{12,4},... | collective-permute-start | bytes 3145736 | tf_op jit(solution)/shard_map/ppermute | solution.py:20
  93.0 2.0 collective-permute-done.13.refs_10_.refs_9_
  99.5 2.3 collective-permute-done.10.refs_19_.refs_18_
  103.0 4.2 %collective-permute-done.11.refs_20_.refs_19_ = bf16[128,1280]{1,0:T(8,128)(2,1)S(1)} collective-permute-done((bf16[128,1280]{1,0:T(8,128)(2,1)S(1)}, bf16[128,1280]{1,0:T(8,128)(2,1)S(1)}, u32[]{:S(2)}, u32[]{:S(2)}) %collective-permute-start.11) | collective-permute-done | bytes 327712 | tf_op jit(solution)/shard_map/ppermute | solution.py:20
  111.0 4.3 %collective-permute-start.55 = (bf16[512,256]{1,0:T(8,128)(2,1)S(1)}, bf16[512,256]{1,0:T(8,128)(2,1)S(1)}, u32[]{:S(2)}, u32[]{:S(2)}) collective-permute-start(bf16[512,256]{1,0:T(8,128)(2,1)S(1)} %slice_bitcast_fusion.10), channel_id=1, source_target_pairs={{1,8},{8,1},{3,10},{10,3},{5,12},{12,5},{7,14},{14,7},{17,24},{24,... | collective-permute-start | bytes 786440 | tf_op jit(solution)/shard_map/ppermute | solution.py:24
  115.3 4.8 %collective-permute-done.55 = bf16[512,256]{1,0:T(8,128)(2,1)S(1)} collective-permute-done((bf16[512,256]{1,0:T(8,128)(2,1)S(1)}, bf16[512,256]{1,0:T(8,128)(2,1)S(1)}, u32[]{:S(2)}, u32[]{:S(2)}) %collective-permute-start.55) | collective-permute-done | bytes 262176 | tf_op jit(solution)/shard_map/ppermute | solution.py:24
  124.2 15.1 %shard_map.82 = (bf16[256,1536]{1,0:T(8,128)(2,1)}, bf16[256,1536]{1,0:T(8,128)(2,1)}, bf16[32,1024]{1,0:T(8,128)(2,1)S(1)}) custom-call(s32[30]{0:T(128)S(1)} %stack.176.index_ref, s32[8]{0:T(128)S(1)} %stack.185.place_ref, f32[8,512]{1,0:T(8,128)S(1)} %squeeze.33.gain_ref, bf16[4,2,512,512]{3,2,1,0:T(8,128)(2,1)} %bitcast.87, bf16[256,2048]{1,0:T(8,128)(2,1)} %copy-done.5, ...), custom_call_target="tpu_custom_call" | custom-call | flops 6442450944 | bytes 18874368 | tf_op jit(solution)/shard_map/pallas_call | solution.py:119
  139.3 5.9 %shard_map.84 = (bf16[256,1024]{1,0:T(8,128)(2,1)S(1)}, bf16[256,1024]{1,0:T(8,128)(2,1)}, bf16[256,1024]{1,0:T(8,128)(2,1)}, bf16[256,1024]{1,0:T(8,128)(2,1)}) custom-call(s32[30]{0:T(128)S(1)} %stack.176.index_ref, bf16[256,1536]{1,0:T(8,128)(2,1)} %get-tuple-element.85.main_ref.before_ref, bf16[256,1536]{1,0:T(8,128)(2,1)} %get-tuple-element.92.main_ref, ...), custom_call_target="tpu_custom_call" | custom-call | flops 1073741824 | bytes 6291456 | tf_op jit(solution)/shard_map/pallas_call | solution.py:246
  146.0 3.6 %collective-permute-start.32 = (bf16[256,1024]{1,0:T(8,128)(2,1)}, bf16[256,1024]{1,0:T(8,128)(2,1)}, u32[]{:S(2)}, u32[]{:S(2)}) collective-permute-start(bf16[256,1024]{1,0:T(8,128)(2,1)} %get-tuple-element.96), channel_id=1, source_target_pairs={{0,4},{2,6},{4,0},{6,2},{1,5},{3,7},{5,1},{7,3},{8,12},{10,14},{12... | collective-permute-start | bytes 1572872 | tf_op jit(solution)/shard_map/ppermute | solution.py:20
  151.1 2.1 collective-permute-start.26
  153.2 1.7 pad_maximum_fusion.5
  154.9 4.7 %collective-permute-start.25 = (bf16[512,512]{1,0:T(8,128)(2,1)}, bf16[512,512]{1,0:T(8,128)(2,1)S(1)}, u32[]{:S(2)}, u32[]{:S(2)}) collective-permute-start(bf16[512,512]{1,0:T(8,128)(2,1)} %param.8), channel_id=1, source_target_pairs={{1,8},{8,1},{3,10},{10,3},{5,12},{12,5},{7,14},{14,7},{17,24},{24,... | collective-permute-start | bytes 1572872 | tf_op jit(solution)/shard_map/ppermute | solution.py:24
  159.6 4.9 %shard_map.83 = (bf16[256,1024]{1,0:T(8,128)(2,1)S(1)}, bf16[256,1024]{1,0:T(8,128)(2,1)S(1)}, bf16[256,1024]{1,0:T(8,128)(2,1)S(1)}, bf16[256,1024]{1,0:T(8,128)(2,1)S(1)}) custom-call(s32[30]{0:T(128)S(1)} %stack.176.index_ref, bf16[32,1024]{1,0:T(8,128)(2,1)S(1)} %collective-permute-done.26.before_ref, ...), custom_call_target="tpu_custom_call" | custom-call | flops 1073741824 | bytes 6291456 | tf_op jit(solution)/shard_map/pallas_call | solution.py:246
  167.3 6.5 %collective-permute-done.31 = bf16[256,1024]{1,0:T(8,128)(2,1)} collective-permute-done((bf16[256,1024]{1,0:T(8,128)(2,1)}, bf16[256,1024]{1,0:T(8,128)(2,1)}, u32[]{:S(2)}, u32[]{:S(2)}) %collective-permute-start.31) | collective-permute-done | bytes 524320 | tf_op jit(solution)/shard_map/ppermute | solution.py:20
  174.7 1.8 add_convert_fusion.3
  176.5 5.6 %collective-permute-start.34 = (bf16[256,512]{1,0:T(8,128)(2,1)S(1)}, bf16[256,512]{1,0:T(8,128)(2,1)S(1)}, u32[]{:S(2)}, u32[]{:S(2)}) collective-permute-start(bf16[256,512]{1,0:T(8,128)(2,1)S(1)} %get-tuple-element.137), channel_id=1, source_target_pairs={{1,8},{8,1},{3,10},{10,3},{5,12},{12,5},{7,14},{14,7},{17,24},{24,... | collective-permute-start | bytes 786440 | tf_op jit(solution)/shard_map/ppermute | solution.py:389
  184.9 3.9 %collective-permute-start.33 = (bf16[256,512]{1,0:T(8,128)(2,1)S(1)}, bf16[256,512]{1,0:T(8,128)(2,1)S(1)}, u32[]{:S(2)}, u32[]{:S(2)}) collective-permute-start(bf16[256,512]{1,0:T(8,128)(2,1)S(1)} %get-tuple-element.138), channel_id=1, source_target_pairs={{1,0},{8,9},{3,2},{10,11},{5,4},{12,13},{7,6},{14,15},{17,16},{24,... | collective-permute-start | bytes 786440 | tf_op jit(solution)/shard_map/ppermute | solution.py:388
  188.9 6.8 %collective-permute-done.29 = bf16[256,1024]{1,0:T(8,128)(2,1)S(1)} collective-permute-done((bf16[256,1024]{1,0:T(8,128)(2,1)S(1)}, bf16[256,1024]{1,0:T(8,128)(2,1)S(1)}, u32[]{:S(2)}, u32[]{:S(2)}) %collective-permute-start.29) | collective-permute-done | bytes 524320 | tf_op jit(solution)/shard_map/ppermute | solution.py:20
  195.7 3.7 %collective-permute-done.33 = bf16[256,512]{1,0:T(8,128)(2,1)S(1)} collective-permute-done((bf16[256,512]{1,0:T(8,128)(2,1)S(1)}, bf16[256,512]{1,0:T(8,128)(2,1)S(1)}, u32[]{:S(2)}, u32[]{:S(2)}) %collective-permute-start.33) | collective-permute-done | bytes 262176 | tf_op jit(solution)/shard_map/ppermute | solution.py:388
  199.9 2.6 collective-permute-start.37
  203.8 5.3 %collective-permute-start.36 = (bf16[256,512]{1,0:T(8,128)(2,1)S(1)}, bf16[256,512]{1,0:T(8,128)(2,1)S(1)}, u32[]{:S(2)}, u32[]{:S(2)}) collective-permute-start(bf16[256,512]{1,0:T(8,128)(2,1)S(1)} %get-tuple-element.136), channel_id=1, source_target_pairs={{1,0},{8,9},{3,2},{10,11},{5,4},{12,13},{7,6},{14,15},{17,16},{24,... | collective-permute-start | bytes 786440 | tf_op jit(solution)/shard_map/ppermute | solution.py:388
  209.3 1.9 collective-permute-start.39
  212.1 13.3 %collective-permute-start.41 = (bf16[256,512]{1,0:T(8,128)(2,1)S(1)}, bf16[256,512]{1,0:T(8,128)(2,1)S(1)}, u32[]{:S(2)}, u32[]{:S(2)}) collective-permute-start(bf16[256,512]{1,0:T(8,128)(2,1)S(1)} %add_convert_fusion.5.refs_8_), channel_id=1, source_target_pairs={{0,4},{2,6},{4,0},{6,2},{1,5},{3,7},{5,1},{7,3},{8,12},{10,14},{12... | collective-permute-start | bytes 786440 | tf_op jit(solution)/shard_map/ppermute | solution.py:20
  225.4 6.4 %collective-permute-done.41.refs_11_ = bf16[256,512]{1,0:T(8,128)(2,1)S(1)} collective-permute-done((bf16[256,512]{1,0:T(8,128)(2,1)S(1)}, bf16[256,512]{1,0:T(8,128)(2,1)S(1)}, u32[]{:S(2)}, u32[]{:S(2)}) %collective-permute-start.41) | collective-permute-done | bytes 262176 | tf_op jit(solution)/shard_map/ppermute | solution.py:20
  236.3 9.7 %collective-permute-done.42.refs_1_ = bf16[256,512]{1,0:T(8,128)(2,1)S(1)} collective-permute-done((bf16[256,512]{1,0:T(8,128)(2,1)S(1)}, bf16[256,512]{1,0:T(8,128)(2,1)S(1)}, u32[]{:S(2)}, u32[]{:S(2)}) %collective-permute-start.42) | collective-permute-done | bytes 262176 | tf_op jit(solution)/shard_map/ppermute | solution.py:20
  247.9 2.6 collective-permute-start.53
  250.6 14.8 %shard_map.85 = (bf16[256,1536]{1,0:T(8,128)(2,1)}, bf16[256,1536]{1,0:T(8,128)(2,1)}, bf16[160,1024]{1,0:T(8,128)(2,1)}) custom-call(s32[30]{0:T(128)S(1)} %stack.176.index_ref, s32[16]{0:T(128)S(1)} %stack.203.place_ref, f32[8,512]{1,0:T(8,128)S(1)} %squeeze.35.gain_ref, bf16[256,512]{1,0:T(8,128)(2,1)S(1)} %add_convert_fusion.4.refs_0_, ...), custom_call_target="tpu_custom_call" | custom-call | flops 6442450944 | bytes 18874368 | tf_op jit(solution)/shard_map/pallas_call | solution.py:119
  265.4 1.9 collective-permute-start.54
  270.7 7.6 %shard_map.86.inner = bf16[256,512]{1,0:T(8,128)(2,1)S(1)} custom-call(bf16[256,1536]{1,0:T(8,128)(2,1)S(1)} %copy-done.3, bf16[256,1536]{1,0:T(8,128)(2,1)S(1)} %copy-done.4, f32[9,512]{1,0:T(8,128)S(1)} %slice.176.feat_ref, f32[128,512]{1,0:T(8,128)S(1)} %slice.177.filter_ref, f32[1,512]{1,0:T(1,128)S(1)} %slice.178.skip_ref), custom_call_target="tpu_custom_call" | custom-call | flops 3221225472 | bytes 3145728 | tf_op jit(solution)/shard_map/pallas_call | solution.py:269
  278.6 7.6 %shard_map.87.inner = bf16[256,512]{1,0:T(8,128)(2,1)S(1)} custom-call(bf16[160,1024]{1,0:T(8,128)(2,1)S(1)} %collective-permute-done.54.before_ref, bf16[256,1536]{1,0:T(8,128)(2,1)S(1)} %copy-done.3, f32[9,512]{1,0:T(8,128)S(1)} %slice.176.feat_ref, f32[128,512]{1,0:T(8,128)S(1)} %slice.177.filter_ref, f32[1,512]{1,0:T(1,128)S(1)} %slice.178.skip_ref), custom_call_target="tpu_custom_call" | custom-call | flops 3221225472 | bytes 3145728 | tf_op jit(solution)/shard_map/pallas_call | solution.py:269
  286.3 4.1 %shard_map.89 = (bf16[4,256,512]{2,1,0:T(8,128)(2,1)S(1)}, bf16[4,256,512]{2,1,0:T(8,128)(2,1)S(1)}) custom-call(s32[30]{0:T(128)S(1)} %stack.176.index_ref, bf16[256,512]{1,0:T(8,128)(2,1)S(1)} %shard_map.86.inner, bf16[16,512,256]{2,1,0:T(8,128)(2,1)} %bitcast.79), custom_call_target="tpu_custom_call" | custom-call | flops 1073741824 | bytes 6291456 | tf_op jit(solution)/shard_map/pallas_call | solution.py:292
  290.4 1.8 collective-permute-start.61
  292.2 4.1 %shard_map.88 = (bf16[4,256,512]{2,1,0:T(8,128)(2,1)S(1)}, bf16[4,256,512]{2,1,0:T(8,128)(2,1)S(1)}) custom-call(s32[30]{0:T(128)S(1)} %stack.176.index_ref, bf16[256,512]{1,0:T(8,128)(2,1)S(1)} %shard_map.87.inner, bf16[16,512,256]{2,1,0:T(8,128)(2,1)} %bitcast.80), custom_call_target="tpu_custom_call" | custom-call | flops 1073741824 | bytes 6291456 | tf_op jit(solution)/shard_map/pallas_call | solution.py:292
  298.5 1.9 collective-permute-start.63
  302.1 2.1 collective-permute-start.58
  304.2 1.8 collective-permute-done.64
  306.9 4.7 %collective-permute-done.63 = bf16[256,512]{1,0:T(8,128)(2,1)S(1)} collective-permute-done((bf16[256,512]{1,0:T(8,128)(2,1)S(1)}, bf16[256,512]{1,0:T(8,128)(2,1)S(1)}, u32[]{:S(2)}, u32[]{:S(2)}) %collective-permute-start.63) | collective-permute-done | bytes 262176 | tf_op jit(solution)/shard_map/ppermute | solution.py:20
  311.5 1.7 collective-permute-done.62
  313.4 3.2 collective-permute-start.65
  317.3 5.5 %collective-permute-done.58 = bf16[256,512]{1,0:T(8,128)(2,1)S(1)} collective-permute-done((bf16[256,512]{1,0:T(8,128)(2,1)S(1)}, bf16[256,512]{1,0:T(8,128)(2,1)S(1)}, u32[]{:S(2)}, u32[]{:S(2)}) %collective-permute-start.58) | collective-permute-done | bytes 262176 | tf_op jit(solution)/shard_map/ppermute | solution.py:20
  323.8 3.0 collective-permute-start.60
  326.8 6.2 %collective-permute-done.60 = bf16[256,512]{1,0:T(8,128)(2,1)S(1)} collective-permute-done((bf16[256,512]{1,0:T(8,128)(2,1)S(1)}, bf16[256,512]{1,0:T(8,128)(2,1)S(1)}, u32[]{:S(2)}, u32[]{:S(2)}) %collective-permute-start.60) | collective-permute-done | bytes 262176 | tf_op jit(solution)/shard_map/ppermute | solution.py:24
  (201 shorter events, 58.0 us)
Async XLA Ops:
  6.5 117.6 %all-gather.7.cloned.1.call-start = ((), (), s32[]{:S(2)}) async-start(), calls=%async_computation | async-start | bytes 5242880 | tf_op jit(solution)/shard_map/all_gather | solution.py:317
  8.3 23.0 %collective-permute-start.4 = (bf16[256,3,512]{0,2,1:T(8,128)(2,1)S(1)}, bf16[256,3,512]{0,2,1:T(8,128)(2,1)}, u32[]{:S(2)}, u32[]{:S(2)}) collective-permute-start(bf16[256,3,512]{0,2,1:T(8,128)(2,1)S(1)} %bitcast.82), channel_id=1, source_target_pairs={{1,8},{8,1},{3,10},{10,3},{5,12},{12,5},{7,14},{14,7},{17,24},{24,... | collective-permute-start | bytes 2359304 | tf_op jit(solution)/shard_map/ppermute | solution.py:24
  14.3 41.4 %collective-permute-start.1 = (bf16[256,2048]{1,0:T(8,128)(2,1)S(1)}, bf16[256,2048]{1,0:T(8,128)(2,1)}, u32[]{:S(2)}, u32[]{:S(2)}) collective-permute-start(bf16[256,2048]{1,0:T(8,128)(2,1)S(1)} %pad_maximum_fusion.refs_1_.refs_0_), channel_id=1, source_target_pairs={{0,64},{64,0},{1,65},{65,1},{2,66},{66,2},{3,67},{67,3},{4,68},{68... | collective-permute-start | bytes 3145736 | tf_op jit(solution)/shard_map/ppermute | solution.py:20
  14.7 41.0 %collective-permute-start.2 = (bf16[256,2048]{1,0:T(8,128)(2,1)S(1)}, bf16[256,2048]{1,0:T(8,128)(2,1)}, u32[]{:S(2)}, u32[]{:S(2)}) collective-permute-start(bf16[256,2048]{1,0:T(8,128)(2,1)S(1)} %pad_maximum_fusion.refs_1_.refs_0_), channel_id=1, source_target_pairs={{0,16},{16,32},{32,48},{48,0},{1,17},{17,33},{33,49},{49,1},{2,18}... | collective-permute-start | bytes 3145736 | tf_op jit(solution)/shard_map/ppermute | solution.py:20
  14.7 41.0 %collective-permute-start.3 = (bf16[256,2048]{1,0:T(8,128)(2,1)S(1)}, bf16[256,2048]{1,0:T(8,128)(2,1)}, u32[]{:S(2)}, u32[]{:S(2)}) collective-permute-start(bf16[256,2048]{1,0:T(8,128)(2,1)S(1)} %pad_maximum_fusion.refs_1_.refs_0_), channel_id=1, source_target_pairs={{0,48},{16,0},{32,16},{48,32},{1,49},{17,1},{33,17},{49,33},{2,50}... | collective-permute-start | bytes 3145736 | tf_op jit(solution)/shard_map/ppermute | solution.py:20
  16.2 39.5 %collective-permute-start = (bf16[512,512]{1,0:T(8,128)(2,1)S(1)}, bf16[512,512]{1,0:T(8,128)(2,1)S(1)}, u32[]{:S(2)}, u32[]{:S(2)}) collective-permute-start(bf16[512,512]{1,0:T(8,128)(2,1)S(1)} %copy-done.16), channel_id=1, source_target_pairs={{0,1},{1,0},{2,3},{3,2},{4,5},{5,4},{6,7},{7,6},{8,9},{9,8},{10,11... | collective-permute-start | bytes 1572872 | tf_op jit(solution)/shard_map/ppermute | solution.py:20
  56.8 193.8 %all-gather.9.cloned.1.call-start = ((), (), s32[]{:S(2)}) async-start(), calls=%async_computation.1 | async-start | bytes 13369344 | tf_op jit(solution)/shard_map/all_gather | solution.py:309
  58.1 27.9 %collective-permute-start.9 = (bf16[2,256,768]{2,1,0:T(8,128)(2,1)S(1)}, bf16[2,256,768]{2,1,0:T(8,128)(2,1)}, u32[]{:S(2)}, u32[]{:S(2)}) collective-permute-start(bf16[2,256,768]{2,1,0:T(8,128)(2,1)S(1)} %pad_maximum_fusion.2), channel_id=1, source_target_pairs={{0,64},{64,0},{1,65},{65,1},{2,66},{66,2},{3,67},{67,3},{4,68},{68... | collective-permute-start | bytes 2359304 | tf_op jit(solution)/shard_map/ppermute | solution.py:20
  59.6 26.4 %collective-permute-start.7 = (bf16[256,1280]{1,0:T(8,128)(2,1)S(1)}, bf16[256,1280]{1,0:T(8,128)(2,1)S(1)}, u32[]{:S(2)}, u32[]{:S(2)}) collective-permute-start(bf16[256,1280]{1,0:T(8,128)(2,1)S(1)} %slice.142), channel_id=1, source_target_pairs={{0,16},{16,32},{32,48},{48,0},{1,17},{17,33},{33,49},{49,1},{2,18}... | collective-permute-start | bytes 1966088 | tf_op jit(solution)/shard_map/ppermute | solution.py:20
  59.7 26.3 %collective-permute-start.8 = (bf16[256,1280]{1,0:T(8,128)(2,1)S(1)}, bf16[256,1280]{1,0:T(8,128)(2,1)}, u32[]{:S(2)}, u32[]{:S(2)}) collective-permute-start(bf16[256,1280]{1,0:T(8,128)(2,1)S(1)} %slice.142), channel_id=1, source_target_pairs={{0,48},{16,0},{32,16},{48,32},{1,49},{17,1},{33,17},{49,33},{2,50}... | collective-permute-start | bytes 1966088 | tf_op jit(solution)/shard_map/ppermute | solution.py:20
  63.3 21.5 %collective-permute-start.5 = (bf16[128,2048]{1,0:T(8,128)(2,1)S(1)}, bf16[128,2048]{1,0:T(8,128)(2,1)S(1)}, u32[]{:S(2)}, u32[]{:S(2)}) collective-permute-start(bf16[128,2048]{1,0:T(8,128)(2,1)S(1)} %slice.140), channel_id=1, source_target_pairs={{0,16},{16,32},{32,48},{48,0},{1,17},{17,33},{33,49},{49,1},{2,18}... | collective-permute-start | bytes 1572872 | tf_op jit(solution)/shard_map/ppermute | solution.py:20
  64.7 21.3 %collective-permute-start.6 = (bf16[128,2048]{1,0:T(8,128)(2,1)S(1)}, bf16[128,2048]{1,0:T(8,128)(2,1)S(1)}, u32[]{:S(2)}, u32[]{:S(2)}) collective-permute-start(bf16[128,2048]{1,0:T(8,128)(2,1)S(1)} %slice.141), channel_id=1, source_target_pairs={{0,48},{16,0},{32,16},{48,32},{1,49},{17,1},{33,17},{49,33},{2,50}... | collective-permute-start | bytes 1572872 | tf_op jit(solution)/shard_map/ppermute | solution.py:20
  88.6 197.7 %all-gather.11.cloned.1.call-start = ((), (), s32[]{:S(2)}) async-start(), calls=%async_computation.2 | async-start | bytes 4456448 | tf_op jit(solution)/shard_map/all_gather | solution.py:309
  95.0 13.6 %collective-permute-start.12 = (bf16[2,128,768]{2,1,0:T(8,128)(2,1)S(1)}, bf16[2,128,768]{2,1,0:T(8,128)(2,1)S(1)}, u32[]{:S(2)}, u32[]{:S(2)}) collective-permute-start(bf16[2,128,768]{2,1,0:T(8,128)(2,1)S(1)} %pad_maximum_fusion.4), channel_id=1, source_target_pairs={{0,64},{64,0},{1,65},{65,1},{2,66},{66,2},{3,67},{67,3},{4,68},{68... | collective-permute-start | bytes 1179656 | tf_op jit(solution)/shard_map/ppermute | solution.py:20
  97.2 10.0 %collective-permute-start.11 = (bf16[128,1280]{1,0:T(8,128)(2,1)S(1)}, bf16[128,1280]{1,0:T(8,128)(2,1)S(1)}, u32[]{:S(2)}, u32[]{:S(2)}) collective-permute-start(bf16[128,1280]{1,0:T(8,128)(2,1)S(1)} %slice.146), channel_id=1, source_target_pairs={{0,48},{16,0},{32,16},{48,32},{1,49},{17,1},{33,17},{49,33},{2,50}... | collective-permute-start | bytes 983048 | tf_op jit(solution)/shard_map/ppermute | solution.py:20
  97.6 13.3 %collective-permute-start.21 = (bf16[2,256,768]{2,1,0:T(8,128)(2,1)}, bf16[2,256,768]{2,1,0:T(8,128)(2,1)S(1)}, u32[]{:S(2)}, u32[]{:S(2)}) collective-permute-start(bf16[2,256,768]{2,1,0:T(8,128)(2,1)} %collective-permute-done.9.refs_9_.refs_8_), channel_id=1, source_target_pairs={{0,8},{8,0},{1,9},{9,1},{2,10},{10,2},{3,11},{11,3},{4,12},{12,4},... | collective-permute-start | bytes 2359304 | tf_op jit(solution)/shard_map/ppermute | solution.py:20
  99.1 11.8 %collective-permute-start.19 = (bf16[256,1280]{1,0:T(8,128)(2,1)S(1)}, bf16[256,1280]{1,0:T(8,128)(2,1)S(1)}, u32[]{:S(2)}, u32[]{:S(2)}) collective-permute-start(bf16[256,1280]{1,0:T(8,128)(2,1)S(1)} %copy-done.11), channel_id=1, source_target_pairs={{0,8},{8,0},{1,9},{9,1},{2,10},{10,2},{3,11},{11,3},{4,12},{12,4},... | collective-permute-start | bytes 1966088 | tf_op jit(solution)/shard_map/ppermute | solution.py:20
  111.0 9.2 %collective-permute-start.55 = (bf16[512,256]{1,0:T(8,128)(2,1)S(1)}, bf16[512,256]{1,0:T(8,128)(2,1)S(1)}, u32[]{:S(2)}, u32[]{:S(2)}) collective-permute-start(bf16[512,256]{1,0:T(8,128)(2,1)S(1)} %slice_bitcast_fusion.10), channel_id=1, source_target_pairs={{1,8},{8,1},{3,10},{10,3},{5,12},{12,5},{7,14},{14,7},{17,24},{24,... | collective-permute-start | bytes 786440 | tf_op jit(solution)/shard_map/ppermute | solution.py:24
  146.0 19.8 %collective-permute-start.32 = (bf16[256,1024]{1,0:T(8,128)(2,1)}, bf16[256,1024]{1,0:T(8,128)(2,1)}, u32[]{:S(2)}, u32[]{:S(2)}) collective-permute-start(bf16[256,1024]{1,0:T(8,128)(2,1)} %get-tuple-element.96), channel_id=1, source_target_pairs={{0,4},{2,6},{4,0},{6,2},{1,5},{3,7},{5,1},{7,3},{8,12},{10,14},{12... | collective-permute-start | bytes 1572872 | tf_op jit(solution)/shard_map/ppermute | solution.py:20
  149.6 24.2 %collective-permute-start.31 = (bf16[256,1024]{1,0:T(8,128)(2,1)}, bf16[256,1024]{1,0:T(8,128)(2,1)}, u32[]{:S(2)}, u32[]{:S(2)}) collective-permute-start(bf16[256,1024]{1,0:T(8,128)(2,1)} %get-tuple-element.95), channel_id=1, source_target_pairs={{0,6},{2,0},{4,2},{6,4},{1,7},{3,1},{5,3},{7,5},{8,14},{10,8},{12,... | collective-permute-start | bytes 1572872 | tf_op jit(solution)/shard_map/ppermute | solution.py:20
  150.0 24.7 %collective-permute-start.30 = (bf16[256,1024]{1,0:T(8,128)(2,1)}, bf16[256,1024]{1,0:T(8,128)(2,1)}, u32[]{:S(2)}, u32[]{:S(2)}) collective-permute-start(bf16[256,1024]{1,0:T(8,128)(2,1)} %get-tuple-element.94), channel_id=1, source_target_pairs={{0,2},{2,4},{4,6},{6,0},{1,3},{3,5},{5,7},{7,1},{8,10},{10,12},{12... | collective-permute-start | bytes 1572872 | tf_op jit(solution)/shard_map/ppermute | solution.py:20
  154.9 27.2 %collective-permute-start.25 = (bf16[512,512]{1,0:T(8,128)(2,1)}, bf16[512,512]{1,0:T(8,128)(2,1)S(1)}, u32[]{:S(2)}, u32[]{:S(2)}) collective-permute-start(bf16[512,512]{1,0:T(8,128)(2,1)} %param.8), channel_id=1, source_target_pairs={{1,8},{8,1},{3,10},{10,3},{5,12},{12,5},{7,14},{14,7},{17,24},{24,... | collective-permute-start | bytes 1572872 | tf_op jit(solution)/shard_map/ppermute | solution.py:24
  164.6 20.3 %collective-permute-start.27 = (bf16[256,1024]{1,0:T(8,128)(2,1)S(1)}, bf16[256,1024]{1,0:T(8,128)(2,1)S(1)}, u32[]{:S(2)}, u32[]{:S(2)}) collective-permute-start(bf16[256,1024]{1,0:T(8,128)(2,1)S(1)} %get-tuple-element.89), channel_id=1, source_target_pairs={{0,2},{2,4},{4,6},{6,0},{1,3},{3,5},{5,7},{7,1},{8,10},{10,12},{12... | collective-permute-start | bytes 1572872 | tf_op jit(solution)/shard_map/ppermute | solution.py:20
  165.8 23.1 %collective-permute-start.28 = (bf16[256,1024]{1,0:T(8,128)(2,1)S(1)}, bf16[256,1024]{1,0:T(8,128)(2,1)S(1)}, u32[]{:S(2)}, u32[]{:S(2)}) collective-permute-start(bf16[256,1024]{1,0:T(8,128)(2,1)S(1)} %get-tuple-element.90), channel_id=1, source_target_pairs={{0,6},{2,0},{4,2},{6,4},{1,7},{3,1},{5,3},{7,5},{8,14},{10,8},{12,... | collective-permute-start | bytes 1572872 | tf_op jit(solution)/shard_map/ppermute | solution.py:20
  173.8 21.9 %collective-permute-start.29 = (bf16[256,1024]{1,0:T(8,128)(2,1)S(1)}, bf16[256,1024]{1,0:T(8,128)(2,1)S(1)}, u32[]{:S(2)}, u32[]{:S(2)}) collective-permute-start(bf16[256,1024]{1,0:T(8,128)(2,1)S(1)} %get-tuple-element.91), channel_id=1, source_target_pairs={{0,4},{2,6},{4,0},{6,2},{1,5},{3,7},{5,1},{7,3},{8,12},{10,14},{12... | collective-permute-start | bytes 1572872 | tf_op jit(solution)/shard_map/ppermute | solution.py:20
  176.5 22.9 %collective-permute-start.34 = (bf16[256,512]{1,0:T(8,128)(2,1)S(1)}, bf16[256,512]{1,0:T(8,128)(2,1)S(1)}, u32[]{:S(2)}, u32[]{:S(2)}) collective-permute-start(bf16[256,512]{1,0:T(8,128)(2,1)S(1)} %get-tuple-element.137), channel_id=1, source_target_pairs={{1,8},{8,1},{3,10},{10,3},{5,12},{12,5},{7,14},{14,7},{17,24},{24,... | collective-permute-start | bytes 786440 | tf_op jit(solution)/shard_map/ppermute | solution.py:389
  182.1 17.3 %collective-permute-start.35 = (bf16[256,512]{1,0:T(8,128)(2,1)S(1)}, bf16[256,512]{1,0:T(8,128)(2,1)S(1)}, u32[]{:S(2)}, u32[]{:S(2)}) collective-permute-start(bf16[256,512]{1,0:T(8,128)(2,1)S(1)} %get-tuple-element.137), channel_id=1, source_target_pairs={{0,8},{9,1},{2,10},{11,3},{4,12},{13,5},{6,14},{15,7},{16,24},{25,... | collective-permute-start | bytes 786440 | tf_op jit(solution)/shard_map/ppermute | solution.py:390
  184.9 14.5 %collective-permute-start.33 = (bf16[256,512]{1,0:T(8,128)(2,1)S(1)}, bf16[256,512]{1,0:T(8,128)(2,1)S(1)}, u32[]{:S(2)}, u32[]{:S(2)}) collective-permute-start(bf16[256,512]{1,0:T(8,128)(2,1)S(1)} %get-tuple-element.138), channel_id=1, source_target_pairs={{1,0},{8,9},{3,2},{10,11},{5,4},{12,13},{7,6},{14,15},{17,16},{24,... | collective-permute-start | bytes 786440 | tf_op jit(solution)/shard_map/ppermute | solution.py:388
  199.9 25.5 %collective-permute-start.37 = (bf16[256,512]{1,0:T(8,128)(2,1)S(1)}, bf16[256,512]{1,0:T(8,128)(2,1)S(1)}, u32[]{:S(2)}, u32[]{:S(2)}) collective-permute-start(bf16[256,512]{1,0:T(8,128)(2,1)S(1)} %get-tuple-element.135), channel_id=1, source_target_pairs={{1,8},{8,1},{3,10},{10,3},{5,12},{12,5},{7,14},{14,7},{17,24},{24,... | collective-permute-start | bytes 786440 | tf_op jit(solution)/shard_map/ppermute | solution.py:389
  203.8 21.6 %collective-permute-start.36 = (bf16[256,512]{1,0:T(8,128)(2,1)S(1)}, bf16[256,512]{1,0:T(8,128)(2,1)S(1)}, u32[]{:S(2)}, u32[]{:S(2)}) collective-permute-start(bf16[256,512]{1,0:T(8,128)(2,1)S(1)} %get-tuple-element.136), channel_id=1, source_target_pairs={{1,0},{8,9},{3,2},{10,11},{5,4},{12,13},{7,6},{14,15},{17,16},{24,... | collective-permute-start | bytes 786440 | tf_op jit(solution)/shard_map/ppermute | solution.py:388
  209.3 16.0 %collective-permute-start.39 = (bf16[256,512]{1,0:T(8,128)(2,1)S(1)}, bf16[256,512]{1,0:T(8,128)(2,1)S(1)}, u32[]{:S(2)}, u32[]{:S(2)}) collective-permute-start(bf16[256,512]{1,0:T(8,128)(2,1)S(1)} %add_convert_fusion.5.refs_8_), channel_id=1, source_target_pairs={{0,2},{2,4},{4,6},{6,0},{1,3},{3,5},{5,7},{7,1},{8,10},{10,12},{12... | collective-permute-start | bytes 786440 | tf_op jit(solution)/shard_map/ppermute | solution.py:20
  211.2 14.2 %collective-permute-start.40 = (bf16[256,512]{1,0:T(8,128)(2,1)S(1)}, bf16[256,512]{1,0:T(8,128)(2,1)S(1)}, u32[]{:S(2)}, u32[]{:S(2)}) collective-permute-start(bf16[256,512]{1,0:T(8,128)(2,1)S(1)} %add_convert_fusion.5.refs_8_), channel_id=1, source_target_pairs={{0,6},{2,0},{4,2},{6,4},{1,7},{3,1},{5,3},{7,5},{8,14},{10,8},{12,... | collective-permute-start | bytes 786440 | tf_op jit(solution)/shard_map/ppermute | solution.py:20
  212.1 19.7 %collective-permute-start.41 = (bf16[256,512]{1,0:T(8,128)(2,1)S(1)}, bf16[256,512]{1,0:T(8,128)(2,1)S(1)}, u32[]{:S(2)}, u32[]{:S(2)}) collective-permute-start(bf16[256,512]{1,0:T(8,128)(2,1)S(1)} %add_convert_fusion.5.refs_8_), channel_id=1, source_target_pairs={{0,4},{2,6},{4,0},{6,2},{1,5},{3,7},{5,1},{7,3},{8,12},{10,14},{12... | collective-permute-start | bytes 786440 | tf_op jit(solution)/shard_map/ppermute | solution.py:20
  225.4 10.5 %collective-permute-start.49 = (bf16[256,512]{1,0:T(8,128)(2,1)S(1)}, bf16[256,512]{1,0:T(8,128)(2,1)S(1)}, u32[]{:S(2)}, u32[]{:S(2)}) collective-permute-start(bf16[256,512]{1,0:T(8,128)(2,1)S(1)} %add_convert_fusion.5.refs_8_), channel_id=1, source_target_pairs={{0,8},{8,0},{1,9},{9,1},{2,10},{10,2},{3,11},{11,3},{4,12},{12,4},... | collective-permute-start | bytes 786440 | tf_op jit(solution)/shard_map/ppermute | solution.py:20
  232.0 14.1 %collective-permute-start.42 = (bf16[256,512]{1,0:T(8,128)(2,1)S(1)}, bf16[256,512]{1,0:T(8,128)(2,1)S(1)}, u32[]{:S(2)}, u32[]{:S(2)}) collective-permute-start(bf16[256,512]{1,0:T(8,128)(2,1)S(1)} %add_convert_fusion.4.refs_0_), channel_id=1, source_target_pairs={{0,2},{2,4},{4,6},{6,0},{1,3},{3,5},{5,7},{7,1},{8,10},{10,12},{12... | collective-permute-start | bytes 786440 | tf_op jit(solution)/shard_map/ppermute | solution.py:20
  233.2 12.8 %collective-permute-start.43 = (bf16[256,512]{1,0:T(8,128)(2,1)S(1)}, bf16[256,512]{1,0:T(8,128)(2,1)S(1)}, u32[]{:S(2)}, u32[]{:S(2)}) collective-permute-start(bf16[256,512]{1,0:T(8,128)(2,1)S(1)} %add_convert_fusion.4.refs_0_), channel_id=1, source_target_pairs={{0,6},{2,0},{4,2},{6,4},{1,7},{3,1},{5,3},{7,5},{8,14},{10,8},{12,... | collective-permute-start | bytes 786440 | tf_op jit(solution)/shard_map/ppermute | solution.py:20
  234.7 11.9 %collective-permute-start.44 = (bf16[256,512]{1,0:T(8,128)(2,1)S(1)}, bf16[256,512]{1,0:T(8,128)(2,1)S(1)}, u32[]{:S(2)}, u32[]{:S(2)}) collective-permute-start(bf16[256,512]{1,0:T(8,128)(2,1)S(1)} %add_convert_fusion.4.refs_0_), channel_id=1, source_target_pairs={{0,4},{2,6},{4,0},{6,2},{1,5},{3,7},{5,1},{7,3},{8,12},{10,14},{12... | collective-permute-start | bytes 786440 | tf_op jit(solution)/shard_map/ppermute | solution.py:20
  235.8 10.8 %collective-permute-start.45 = (bf16[256,512]{1,0:T(8,128)(2,1)S(1)}, bf16[256,512]{1,0:T(8,128)(2,1)S(1)}, u32[]{:S(2)}, u32[]{:S(2)}) collective-permute-start(bf16[256,512]{1,0:T(8,128)(2,1)S(1)} %add_convert_fusion.4.refs_0_), channel_id=1, source_target_pairs={{0,8},{8,0},{1,9},{9,1},{2,10},{10,2},{3,11},{11,3},{4,12},{12,4},... | collective-permute-start | bytes 786440 | tf_op jit(solution)/shard_map/ppermute | solution.py:20
  235.8 11.3 %collective-permute-start.50 = (bf16[256,512]{1,0:T(8,128)(2,1)S(1)}, bf16[256,512]{1,0:T(8,128)(2,1)S(1)}, u32[]{:S(2)}, u32[]{:S(2)}) collective-permute-start(bf16[256,512]{1,0:T(8,128)(2,1)S(1)} %collective-permute-done.39.refs_9_), channel_id=1, source_target_pairs={{0,8},{8,0},{1,9},{9,1},{2,10},{10,2},{3,11},{11,3},{4,12},{12,4},... | collective-permute-start | bytes 786440 | tf_op jit(solution)/shard_map/ppermute | solution.py:20
  247.9 19.5 %collective-permute-start.53 = (f32[138,512]{1,0:T(8,128)S(1)}, f32[138,512]{1,0:T(8,128)}, u32[]{:S(2)}, u32[]{:S(2)}) collective-permute-start(f32[138,512]{1,0:T(8,128)S(1)} %copy-done.18), channel_id=1, source_target_pairs={{1,8},{8,1},{3,10},{10,3},{5,12},{12,5},{7,14},{14,7},{17,24},{24,... | collective-permute-start | bytes 847880 | tf_op jit(solution)/shard_map/ppermute | solution.py:24
  265.4 13.2 %collective-permute-start.54 = (bf16[160,1024]{1,0:T(8,128)(2,1)}, bf16[160,1024]{1,0:T(8,128)(2,1)S(1)}, u32[]{:S(2)}, u32[]{:S(2)}) collective-permute-start(bf16[160,1024]{1,0:T(8,128)(2,1)} %get-tuple-element.115), channel_id=1, source_target_pairs={{0,1},{1,16},{16,17},{17,32},{32,33},{33,48},{48,49},{49,64},{64,6... | collective-permute-start | bytes 983048 | tf_op jit(solution)/shard_map/ppermute | solution.py:30
  298.5 13.1 %collective-permute-start.63 = (bf16[256,512]{1,0:T(8,128)(2,1)S(1)}, bf16[256,512]{1,0:T(8,128)(2,1)S(1)}, u32[]{:S(2)}, u32[]{:S(2)}) collective-permute-start(bf16[256,512]{1,0:T(8,128)(2,1)S(1)} %get-tuple-element.134), channel_id=1, source_target_pairs={{0,6},{2,0},{4,2},{6,4},{1,7},{3,1},{5,3},{7,5},{8,14},{10,8},{12,... | collective-permute-start | bytes 786440 | tf_op jit(solution)/shard_map/ppermute | solution.py:20
  300.3 12.9 %collective-permute-start.62 = (bf16[256,512]{1,0:T(8,128)(2,1)S(1)}, bf16[256,512]{1,0:T(8,128)(2,1)S(1)}, u32[]{:S(2)}, u32[]{:S(2)}) collective-permute-start(bf16[256,512]{1,0:T(8,128)(2,1)S(1)} %get-tuple-element.132), channel_id=1, source_target_pairs={{0,2},{2,4},{4,6},{6,0},{1,3},{3,5},{5,7},{7,1},{8,10},{10,12},{12... | collective-permute-start | bytes 786440 | tf_op jit(solution)/shard_map/ppermute | solution.py:20
  300.7 16.6 %collective-permute-start.59 = (bf16[256,512]{1,0:T(8,128)(2,1)S(1)}, bf16[256,512]{1,0:T(8,128)(2,1)S(1)}, u32[]{:S(2)}, u32[]{:S(2)}) collective-permute-start(bf16[256,512]{1,0:T(8,128)(2,1)S(1)} %get-tuple-element.130), channel_id=1, source_target_pairs={{0,4},{2,6},{4,0},{6,2},{1,5},{3,7},{5,1},{7,3},{8,12},{10,14},{12... | collective-permute-start | bytes 786440 | tf_op jit(solution)/shard_map/ppermute | solution.py:20
  302.1 20.6 %collective-permute-start.58 = (bf16[256,512]{1,0:T(8,128)(2,1)S(1)}, bf16[256,512]{1,0:T(8,128)(2,1)S(1)}, u32[]{:S(2)}, u32[]{:S(2)}) collective-permute-start(bf16[256,512]{1,0:T(8,128)(2,1)S(1)} %get-tuple-element.131), channel_id=1, source_target_pairs={{0,6},{2,0},{4,2},{6,4},{1,7},{3,1},{5,3},{7,5},{8,14},{10,8},{12,... | collective-permute-start | bytes 786440 | tf_op jit(solution)/shard_map/ppermute | solution.py:20
  306.0 17.7 %collective-permute-start.57 = (bf16[256,512]{1,0:T(8,128)(2,1)S(1)}, bf16[256,512]{1,0:T(8,128)(2,1)S(1)}, u32[]{:S(2)}, u32[]{:S(2)}) collective-permute-start(bf16[256,512]{1,0:T(8,128)(2,1)S(1)} %get-tuple-element.129), channel_id=1, source_target_pairs={{0,2},{2,4},{4,6},{6,0},{1,3},{3,5},{5,7},{7,1},{8,10},{10,12},{12... | collective-permute-start | bytes 786440 | tf_op jit(solution)/shard_map/ppermute | solution.py:20
  313.4 13.4 %collective-permute-start.65 = (bf16[256,512]{1,0:T(8,128)(2,1)S(1)}, bf16[256,512]{1,0:T(8,128)(2,1)S(1)}, u32[]{:S(2)}, u32[]{:S(2)}) collective-permute-start(bf16[256,512]{1,0:T(8,128)(2,1)S(1)} %fusion.3), channel_id=1, source_target_pairs={{1,8},{8,1},{3,10},{10,3},{5,12},{12,5},{7,14},{14,7},{17,24},{24,... | collective-permute-start | bytes 786440 | tf_op jit(solution)/shard_map/ppermute | solution.py:24
  323.8 9.2 %collective-permute-start.60 = (bf16[256,512]{1,0:T(8,128)(2,1)S(1)}, bf16[256,512]{1,0:T(8,128)(2,1)S(1)}, u32[]{:S(2)}, u32[]{:S(2)}) collective-permute-start(bf16[256,512]{1,0:T(8,128)(2,1)S(1)} %fusion.7), channel_id=1, source_target_pairs={{1,8},{8,1},{3,10},{10,3},{5,12},{12,5},{7,14},{14,7},{17,24},{24,... | collective-permute-start | bytes 786440 | tf_op jit(solution)/shard_map/ppermute | solution.py:24
  (45 other events, 534.6 us)
Sparse Core Ops, SparseCore 0:
  56.9 50.7 all-gather.6
  109.9 103.2 all-gather.8
  215.3 55.6 all-gather.10
where the time goes:
time: 348 us; the launch traced here: 341 us
  waiting for transfers between devices  133 us (38%)
  starting transfers between devices  103 us (30%)
  Pallas kernels  64.2 us (18%)
  local copies, waits for them, and re-layouts  15.8 us (5%)
  between operations  14.2 us (4%)
  other arithmetic  11.3 us (3%)
    ppermute x52, waiting for transfers between devices, shift(): lax.ppermute(value, axis, [(i, (i + by) % size) for i in range(size)])  102 us
    ppermute x52, starting transfers between devices, shift(): lax.ppermute(value, axis, [(i, (i + by) % size) for i in range(size)])  55.5 us
    pallas_call x2, Pallas kernels, project_in(): pl.pallas_call(functools.partial(in_kernel, moves, len(pieces), halo), ou...  29.9 us
    ppermute x6, waiting for transfers between devices, swap(): moved = lax.ppermute(value, ('core', 'xh'), [(1, 2), (2, 1)])  26.1 us
    ppermute x6, starting transfers between devices, swap(): moved = lax.ppermute(value, ('core', 'xh'), [(1, 2), (2, 1)])  23.1 us
    pallas_call x2, Pallas kernels, filtered(): pl.pallas_call(functools.partial(filter_kernel, halo, length), out_shape=...  15.2 us
    pallas_call x2, Pallas kernels, mix_out(): pl.pallas_call(functools.partial(mix_kernel, moves, halo, length, len(out...  10.8 us
    ppermute x2, starting transfers between devices, over_z(): lax.ppermute(mine, ('core', 'xh'), [(1, 0), (2, 3)])  9.22 us
  transfers between devices with their start and end apart: 69, of which 29 were waited for; matrix products, arithmetic and copies ran while one was open for 6% of the time, Pallas kernels for 18%

commit v1 on v0

--- a/solution.py
+++ b/solution.py
@@ -311,23 +311,25 @@
     side_by_side = lambda w, o: jnp.concatenate([w.reshape(256, 1536), o[:256], o[256:]], axis=1)
 
     m = side_by_side(in_weight[0], out_weight[0])
-    hidden_x, m_xl, m_up, m_down, w1 = together(
-        shift(hidden, "xh", 1), shift(m, "xl", 1), shift(m, "y", 1), shift(m, "y", -1), swap(in_weight[1])
+    m_up, m_down, m_xl, hidden_x = together(
+        shift(m, "y", 1), shift(m, "y", -1), shift(m, "xl", 1), shift(hidden, "xh", 1)
     )
     whole = by_rows(lax.all_gather(by_rows(jnp.stack([hidden, hidden_x])), "z", axis=0, tiled=False))
     most = m_xl[:, :CUT]
+    far_top = shift(m_up[:128], "y", 1)
     far_top, far_low, most_up, most_down, rest = together(
-        shift(m_up[:128], "y", 1),
+        far_top,
         shift(m_down[128:], "y", -1),
         shift(most, "y", 1),
         shift(most, "y", -1),
         shift(jnp.stack([m_up[:, CUT:], m_down[:, CUT:]]), "xl", 1),
     )
     early = [m, m_xl, m_up, m_down, far_top, far_low, most_up, most_down, rest]
-    most_top, most_low, rest_far, *early_other = together(
+    most_top, most_low, rest_far, w1, *early_other = together(
         shift(most_up[:128], "y", 1),
         shift(most_down[128:], "y", -1),
         shift(jnp.stack([far_top[:, CUT:], far_low[:, CUT:]]), "xl", 1),
+        swap(after(in_weight[1], rest)),
         *[other_core(v) for v in early],
     )
     late = [most_top, most_low, rest_far]
@@ -360,7 +362,7 @@
     q_index = jnp.stack(slots).astype(jnp.int32)
     q_list = w_list
 
-    w1 = gather(after(w1.reshape(256, 1536), rest), ("xh", "xl", "y"))
+    w1 = gather(w1.reshape(256, 1536), ("xh", "xl", "y"))
     o1 = gather(swap(after(out_weight[1], rest_far)), ("xh", "xl", "y"))
     small = jnp.concatenate([feat_filter[1].reshape(9, 512), skip_gain[1:2], mr_filter], axis=0)
 

time: 348 us -> 352 us (1.011)
  the two profiles are of different devices: /device:TPU:25 before, /device:TPU:1 now
where the time goes in v1:
time: 352 us; the launch traced here: 345 us
  waiting for transfers between devices  124 us (35%)
  starting transfers between devices  111 us (32%)
  Pallas kernels  63.8 us (18%)
  local copies, waits for them, and re-layouts  19.2 us (5%)
  between operations  14.1 us (4%)
  other arithmetic  13.1 us (4%)
    ppermute x52, waiting for transfers between devices, shift(): lax.ppermute(value, axis, [(i, (i + by) % size) for i in range(size)])  110 us
    ppermute x52, starting transfers between devices, shift(): lax.ppermute(value, axis, [(i, (i + by) % size) for i in range(size)])  60.2 us
    pallas_call x2, Pallas kernels, project_in(): pl.pallas_call(functools.partial(in_kernel, moves, len(pieces), halo), ou...  29.5 us
    ppermute x6, starting transfers between devices, swap(): moved = lax.ppermute(value, ('core', 'xh'), [(1, 2), (2, 1)])  23.7 us
    pallas_call x2, Pallas kernels, filtered(): pl.pallas_call(functools.partial(filter_kernel, halo, length), out_shape=...  15.2 us
    pallas_call x2, Pallas kernels, mix_out(): pl.pallas_call(functools.partial(mix_kernel, moves, halo, length, len(out...  10.9 us
    ppermute x2, starting transfers between devices, over_z(): lax.ppermute(mine, ('core', 'xh'), [(1, 0), (2, 3)])  10.4 us
    ppermute x2, starting transfers between devices, over_z(): lax.ppermute(others, ('core', 'xh'), [(1, 2), (2, 1)])  9.44 us
  transfers between devices with their start and end apart: 69, of which 21 were waited for; matrix products, arithmetic and copies ran while one was open for 6% of the time, Pallas kernels for 17%

profile of v1, /device:TPU:1, one launch (start us, length us, event | category | flops | bytes accessed | tf_op | source)
XLA Modules:
  0.0 344.9 jit_solution(11213685480587138654)
XLA Ops:
  8.2 2.4 fusion.8
  12.2 2.2 collective-permute-start
  17.1 2.5 collective-permute-start.3
  19.6 33.3 %collective-permute-done.3 = bf16[512,512]{1,0:T(8,128)(2,1)S(1)} collective-permute-done((bf16[512,512]{1,0:T(8,128)(2,1)S(1)}, bf16[512,512]{1,0:T(8,128)(2,1)S(1)}, u32[]{:S(2)}, u32[]{:S(2)}) %collective-permute-start.3) | collective-permute-done | bytes 524320 | tf_op jit(solution)/shard_map/ppermute | solution.py:20
  55.3 2.7 collective-permute-start.7
  60.2 2.7 collective-permute-start.5
  65.2 16.9 %collective-permute-done.4.refs_5_.refs_4_ = bf16[128,2048]{1,0:T(8,128)(2,1)S(1)} collective-permute-done((bf16[128,2048]{1,0:T(8,128)(2,1)S(1)}, bf16[128,2048]{1,0:T(8,128)(2,1)S(1)}, u32[]{:S(2)}, u32[]{:S(2)}) %collective-permute-start.4) | collective-permute-done | bytes 524320 | tf_op jit(solution)/shard_map/ppermute | solution.py:20
  82.0 2.8 collective-permute-start.13
  85.5 2.3 copy.22
  87.8 2.7 collective-permute-start.12
  91.7 2.7 collective-permute-start.10
  94.8 7.6 %collective-permute-done.9.refs_19_.refs_18_ = bf16[128,1280]{1,0:T(8,128)(2,1)S(1)} collective-permute-done((bf16[128,1280]{1,0:T(8,128)(2,1)S(1)}, bf16[128,1280]{1,0:T(8,128)(2,1)S(1)}, u32[]{:S(2)}, u32[]{:S(2)}) %collective-permute-start.9) | collective-permute-done | bytes 327712 | tf_op jit(solution)/shard_map/ppermute | solution.py:20
  102.9 5.9 %collective-permute-done.11.refs_21_.refs_20_ = bf16[2,128,768]{2,1,0:T(8,128)(2,1)S(1)} collective-permute-done((bf16[2,128,768]{2,1,0:T(8,128)(2,1)S(1)}, bf16[2,128,768]{2,1,0:T(8,128)(2,1)S(1)}, u32[]{:S(2)}, u32[]{:S(2)}) %collective-permute-start.11) | collective-permute-done | bytes 393248 | tf_op jit(solution)/shard_map/ppermute | solution.py:20
  109.3 2.1 broadcast_select_fusion
  111.7 2.4 copy.18
  114.1 5.4 %collective-permute-start.55 = (bf16[512,256]{1,0:T(8,128)(2,1)S(1)}, bf16[512,256]{1,0:T(8,128)(2,1)S(1)}, u32[]{:S(2)}, u32[]{:S(2)}) collective-permute-start(bf16[512,256]{1,0:T(8,128)(2,1)S(1)} %slice_bitcast_fusion.10), channel_id=1, source_target_pairs={{1,8},{8,1},{3,10},{10,3},{5,12},{12,5},{7,14},{14,7},{17,24},{24,... | collective-permute-start | bytes 786440 | tf_op jit(solution)/shard_map/ppermute | solution.py:24
  119.6 4.0 %collective-permute-done.55 = bf16[512,256]{1,0:T(8,128)(2,1)S(1)} collective-permute-done((bf16[512,256]{1,0:T(8,128)(2,1)S(1)}, bf16[512,256]{1,0:T(8,128)(2,1)S(1)}, u32[]{:S(2)}, u32[]{:S(2)}) %collective-permute-start.55) | collective-permute-done | bytes 262176 | tf_op jit(solution)/shard_map/ppermute | solution.py:24
  127.7 14.9 %shard_map.82 = (bf16[256,1536]{1,0:T(8,128)(2,1)}, bf16[256,1536]{1,0:T(8,128)(2,1)}, bf16[32,1024]{1,0:T(8,128)(2,1)S(1)}) custom-call(s32[30]{0:T(128)S(1)} %stack.176.index_ref, s32[8]{0:T(128)S(1)} %stack.185.place_ref, f32[8,512]{1,0:T(8,128)S(1)} %squeeze.33.gain_ref, bf16[4,2,512,512]{3,2,1,0:T(8,128)(2,1)} %bitcast.87, bf16[256,2048]{1,0:T(8,128)(2,1)} %copy-done.5, ...), custom_call_target="tpu_custom_call" | custom-call | flops 6442450944 | bytes 18874368 | tf_op jit(solution)/shard_map/pallas_call | solution.py:119
  142.6 5.9 %shard_map.84 = (bf16[256,1024]{1,0:T(8,128)(2,1)S(1)}, bf16[256,1024]{1,0:T(8,128)(2,1)}, bf16[256,1024]{1,0:T(8,128)(2,1)}, bf16[256,1024]{1,0:T(8,128)(2,1)}) custom-call(s32[30]{0:T(128)S(1)} %stack.176.index_ref, bf16[256,1536]{1,0:T(8,128)(2,1)} %get-tuple-element.86.main_ref.before_ref, bf16[256,1536]{1,0:T(8,128)(2,1)} %get-tuple-element.93.main_ref, ...), custom_call_target="tpu_custom_call" | custom-call | flops 1073741824 | bytes 6291456 | tf_op jit(solution)/shard_map/pallas_call | solution.py:246
  149.3 3.6 %collective-permute-start.32 = (bf16[256,1024]{1,0:T(8,128)(2,1)}, bf16[256,1024]{1,0:T(8,128)(2,1)}, u32[]{:S(2)}, u32[]{:S(2)}) collective-permute-start(bf16[256,1024]{1,0:T(8,128)(2,1)} %get-tuple-element.97), channel_id=1, source_target_pairs={{0,4},{2,6},{4,0},{6,2},{1,5},{3,7},{5,1},{7,3},{8,12},{10,14},{12... | collective-permute-start | bytes 1572872 | tf_op jit(solution)/shard_map/ppermute | solution.py:20
  154.4 2.8 collective-permute-start.26
  158.9 4.6 %collective-permute-start.25 = (bf16[512,512]{1,0:T(8,128)(2,1)}, bf16[512,512]{1,0:T(8,128)(2,1)S(1)}, u32[]{:S(2)}, u32[]{:S(2)}) collective-permute-start(bf16[512,512]{1,0:T(8,128)(2,1)} %param.8), channel_id=1, source_target_pairs={{1,8},{8,1},{3,10},{10,3},{5,12},{12,5},{7,14},{14,7},{17,24},{24,... | collective-permute-start | bytes 1572872 | tf_op jit(solution)/shard_map/ppermute | solution.py:24
  163.6 5.0 %shard_map.83 = (bf16[256,1024]{1,0:T(8,128)(2,1)S(1)}, bf16[256,1024]{1,0:T(8,128)(2,1)S(1)}, bf16[256,1024]{1,0:T(8,128)(2,1)S(1)}, bf16[256,1024]{1,0:T(8,128)(2,1)S(1)}) custom-call(s32[30]{0:T(128)S(1)} %stack.176.index_ref, bf16[32,1024]{1,0:T(8,128)(2,1)S(1)} %collective-permute-done.26.before_ref, ...), custom_call_target="tpu_custom_call" | custom-call | flops 1073741824 | bytes 6291456 | tf_op jit(solution)/shard_map/pallas_call | solution.py:246
  171.3 5.8 %collective-permute-done.31 = bf16[256,1024]{1,0:T(8,128)(2,1)} collective-permute-done((bf16[256,1024]{1,0:T(8,128)(2,1)}, bf16[256,1024]{1,0:T(8,128)(2,1)}, u32[]{:S(2)}, u32[]{:S(2)}) %collective-permute-start.31) | collective-permute-done | bytes 524320 | tf_op jit(solution)/shard_map/ppermute | solution.py:20
  179.8 6.8 %collective-permute-start.34 = (bf16[256,512]{1,0:T(8,128)(2,1)S(1)}, bf16[256,512]{1,0:T(8,128)(2,1)S(1)}, u32[]{:S(2)}, u32[]{:S(2)}) collective-permute-start(bf16[256,512]{1,0:T(8,128)(2,1)S(1)} %get-tuple-element.137), channel_id=1, source_target_pairs={{1,8},{8,1},{3,10},{10,3},{5,12},{12,5},{7,14},{14,7},{17,24},{24,... | collective-permute-start | bytes 786440 | tf_op jit(solution)/shard_map/ppermute | solution.py:391
  188.2 5.1 %collective-permute-start.33 = (bf16[256,512]{1,0:T(8,128)(2,1)S(1)}, bf16[256,512]{1,0:T(8,128)(2,1)S(1)}, u32[]{:S(2)}, u32[]{:S(2)}) collective-permute-start(bf16[256,512]{1,0:T(8,128)(2,1)S(1)} %get-tuple-element.138), channel_id=1, source_target_pairs={{1,0},{8,9},{3,2},{10,11},{5,4},{12,13},{7,6},{14,15},{17,16},{24,... | collective-permute-start | bytes 786440 | tf_op jit(solution)/shard_map/ppermute | solution.py:390
  193.4 5.7 %collective-permute-done.29 = bf16[256,1024]{1,0:T(8,128)(2,1)S(1)} collective-permute-done((bf16[256,1024]{1,0:T(8,128)(2,1)S(1)}, bf16[256,1024]{1,0:T(8,128)(2,1)S(1)}, u32[]{:S(2)}, u32[]{:S(2)}) %collective-permute-start.29) | collective-permute-done | bytes 524320 | tf_op jit(solution)/shard_map/ppermute | solution.py:20
  199.1 4.8 %collective-permute-done.33 = bf16[256,512]{1,0:T(8,128)(2,1)S(1)} collective-permute-done((bf16[256,512]{1,0:T(8,128)(2,1)S(1)}, bf16[256,512]{1,0:T(8,128)(2,1)S(1)}, u32[]{:S(2)}, u32[]{:S(2)}) %collective-permute-start.33) | collective-permute-done | bytes 262176 | tf_op jit(solution)/shard_map/ppermute | solution.py:390
  204.4 2.6 collective-permute-start.37
  208.3 5.3 %collective-permute-start.36 = (bf16[256,512]{1,0:T(8,128)(2,1)S(1)}, bf16[256,512]{1,0:T(8,128)(2,1)S(1)}, u32[]{:S(2)}, u32[]{:S(2)}) collective-permute-start(bf16[256,512]{1,0:T(8,128)(2,1)S(1)} %get-tuple-element.136), channel_id=1, source_target_pairs={{1,0},{8,9},{3,2},{10,11},{5,4},{12,13},{7,6},{14,15},{17,16},{24,... | collective-permute-start | bytes 786440 | tf_op jit(solution)/shard_map/ppermute | solution.py:390
  216.6 12.9 %collective-permute-start.41 = (bf16[256,512]{1,0:T(8,128)(2,1)S(1)}, bf16[256,512]{1,0:T(8,128)(2,1)S(1)}, u32[]{:S(2)}, u32[]{:S(2)}) collective-permute-start(bf16[256,512]{1,0:T(8,128)(2,1)S(1)} %add_convert_fusion.5.refs_8_), channel_id=1, source_target_pairs={{0,4},{2,6},{4,0},{6,2},{1,5},{3,7},{5,1},{7,3},{8,12},{10,14},{12... | collective-permute-start | bytes 786440 | tf_op jit(solution)/shard_map/ppermute | solution.py:20
  229.5 6.7 %collective-permute-done.41.refs_11_ = bf16[256,512]{1,0:T(8,128)(2,1)S(1)} collective-permute-done((bf16[256,512]{1,0:T(8,128)(2,1)S(1)}, bf16[256,512]{1,0:T(8,128)(2,1)S(1)}, u32[]{:S(2)}, u32[]{:S(2)}) %collective-permute-start.41) | collective-permute-done | bytes 262176 | tf_op jit(solution)/shard_map/ppermute | solution.py:20
  236.9 2.3 collective-permute-start.43
  239.7 10.9 %collective-permute-done.42.refs_1_ = bf16[256,512]{1,0:T(8,128)(2,1)S(1)} collective-permute-done((bf16[256,512]{1,0:T(8,128)(2,1)S(1)}, bf16[256,512]{1,0:T(8,128)(2,1)S(1)}, u32[]{:S(2)}, u32[]{:S(2)}) %collective-permute-start.42) | collective-permute-done | bytes 262176 | tf_op jit(solution)/shard_map/ppermute | solution.py:20
  252.4 2.6 collective-permute-start.53
  255.1 14.6 %shard_map.85 = (bf16[256,1536]{1,0:T(8,128)(2,1)}, bf16[256,1536]{1,0:T(8,128)(2,1)}, bf16[160,1024]{1,0:T(8,128)(2,1)}) custom-call(s32[30]{0:T(128)S(1)} %stack.176.index_ref, s32[16]{0:T(128)S(1)} %stack.203.place_ref, f32[8,512]{1,0:T(8,128)S(1)} %squeeze.35.gain_ref, bf16[256,512]{1,0:T(8,128)(2,1)S(1)} %add_convert_fusion.4.refs_0_, ...), custom_call_target="tpu_custom_call" | custom-call | flops 6442450944 | bytes 18874368 | tf_op jit(solution)/shard_map/pallas_call | solution.py:119
  274.6 7.6 %shard_map.86.inner = bf16[256,512]{1,0:T(8,128)(2,1)S(1)} custom-call(bf16[256,1536]{1,0:T(8,128)(2,1)S(1)} %copy-done.3, bf16[256,1536]{1,0:T(8,128)(2,1)S(1)} %copy-done.4, f32[9,512]{1,0:T(8,128)S(1)} %slice.176.feat_ref, f32[128,512]{1,0:T(8,128)S(1)} %slice.177.filter_ref, f32[1,512]{1,0:T(1,128)S(1)} %slice.178.skip_ref), custom_call_target="tpu_custom_call" | custom-call | flops 3221225472 | bytes 3145728 | tf_op jit(solution)/shard_map/pallas_call | solution.py:269
  282.3 7.6 %shard_map.87.inner = bf16[256,512]{1,0:T(8,128)(2,1)S(1)} custom-call(bf16[160,1024]{1,0:T(8,128)(2,1)S(1)} %collective-permute-done.54.before_ref, bf16[256,1536]{1,0:T(8,128)(2,1)S(1)} %copy-done.3, f32[9,512]{1,0:T(8,128)S(1)} %slice.176.feat_ref, f32[128,512]{1,0:T(8,128)S(1)} %slice.177.filter_ref, f32[1,512]{1,0:T(1,128)S(1)} %slice.178.skip_ref), custom_call_target="tpu_custom_call" | custom-call | flops 3221225472 | bytes 3145728 | tf_op jit(solution)/shard_map/pallas_call | solution.py:269
  289.9 4.1 %shard_map.89 = (bf16[4,256,512]{2,1,0:T(8,128)(2,1)S(1)}, bf16[4,256,512]{2,1,0:T(8,128)(2,1)S(1)}) custom-call(s32[30]{0:T(128)S(1)} %stack.176.index_ref, bf16[256,512]{1,0:T(8,128)(2,1)S(1)} %shard_map.86.inner, bf16[16,512,256]{2,1,0:T(8,128)(2,1)} %bitcast.78), custom_call_target="tpu_custom_call" | custom-call | flops 1073741824 | bytes 6291456 | tf_op jit(solution)/shard_map/pallas_call | solution.py:292
  294.0 2.5 collective-permute-start.61
  296.5 4.1 %shard_map.88 = (bf16[4,256,512]{2,1,0:T(8,128)(2,1)S(1)}, bf16[4,256,512]{2,1,0:T(8,128)(2,1)S(1)}) custom-call(s32[30]{0:T(128)S(1)} %stack.176.index_ref, bf16[256,512]{1,0:T(8,128)(2,1)S(1)} %shard_map.87.inner, bf16[16,512,256]{2,1,0:T(8,128)(2,1)} %bitcast.79), custom_call_target="tpu_custom_call" | custom-call | flops 1073741824 | bytes 6291456 | tf_op jit(solution)/shard_map/pallas_call | solution.py:292
  301.3 2.5 collective-permute-start.63
  306.6 2.1 collective-permute-start.58
  310.5 5.4 %collective-permute-done.63 = bf16[256,512]{1,0:T(8,128)(2,1)S(1)} collective-permute-done((bf16[256,512]{1,0:T(8,128)(2,1)S(1)}, bf16[256,512]{1,0:T(8,128)(2,1)S(1)}, u32[]{:S(2)}, u32[]{:S(2)}) %collective-permute-start.63) | collective-permute-done | bytes 262176 | tf_op jit(solution)/shard_map/ppermute | solution.py:20
  317.6 4.2 %collective-permute-start.65 = (bf16[256,512]{1,0:T(8,128)(2,1)S(1)}, bf16[256,512]{1,0:T(8,128)(2,1)S(1)}, u32[]{:S(2)}, u32[]{:S(2)}) collective-permute-start(bf16[256,512]{1,0:T(8,128)(2,1)S(1)} %fusion.3), channel_id=1, source_target_pairs={{1,8},{8,1},{3,10},{10,3},{5,12},{12,5},{7,14},{14,7},{17,24},{24,... | collective-permute-start | bytes 786440 | tf_op jit(solution)/shard_map/ppermute | solution.py:24
  321.8 5.4 %collective-permute-done.58 = bf16[256,512]{1,0:T(8,128)(2,1)S(1)} collective-permute-done((bf16[256,512]{1,0:T(8,128)(2,1)S(1)}, bf16[256,512]{1,0:T(8,128)(2,1)S(1)}, u32[]{:S(2)}, u32[]{:S(2)}) %collective-permute-start.58) | collective-permute-done | bytes 262176 | tf_op jit(solution)/shard_map/ppermute | solution.py:20
  328.1 4.1 %collective-permute-start.60 = (bf16[256,512]{1,0:T(8,128)(2,1)S(1)}, bf16[256,512]{1,0:T(8,128)(2,1)S(1)}, u32[]{:S(2)}, u32[]{:S(2)}) collective-permute-start(bf16[256,512]{1,0:T(8,128)(2,1)S(1)} %fusion.7), channel_id=1, source_target_pairs={{1,8},{8,1},{3,10},{10,3},{5,12},{12,5},{7,14},{14,7},{17,24},{24,... | collective-permute-start | bytes 786440 | tf_op jit(solution)/shard_map/ppermute | solution.py:24
  332.2 5.0 %collective-permute-done.60 = bf16[256,512]{1,0:T(8,128)(2,1)S(1)} collective-permute-done((bf16[256,512]{1,0:T(8,128)(2,1)S(1)}, bf16[256,512]{1,0:T(8,128)(2,1)S(1)}, u32[]{:S(2)}, u32[]{:S(2)}) %collective-permute-start.60) | collective-permute-done | bytes 262176 | tf_op jit(solution)/shard_map/ppermute | solution.py:24
  (183 shorter events, 52.6 us)
Async XLA Ops:
  6.5 121.1 %all-gather.7.cloned.1.call-start = ((), (), s32[]{:S(2)}) async-start(), calls=%async_computation | async-start | bytes 5242880 | tf_op jit(solution)/shard_map/all_gather | solution.py:317
  12.2 40.7 %collective-permute-start = (bf16[256,2048]{1,0:T(8,128)(2,1)S(1)}, bf16[256,2048]{1,0:T(8,128)(2,1)}, u32[]{:S(2)}, u32[]{:S(2)}) collective-permute-start(bf16[256,2048]{1,0:T(8,128)(2,1)S(1)} %pad_maximum_fusion.refs_1_.refs_0_), channel_id=1, source_target_pairs={{0,16},{16,32},{32,48},{48,0},{1,17},{17,33},{33,49},{49,1},{2,18}... | collective-permute-start | bytes 3145736 | tf_op jit(solution)/shard_map/ppermute | solution.py:20
  14.4 38.5 %collective-permute-start.1 = (bf16[256,2048]{1,0:T(8,128)(2,1)S(1)}, bf16[256,2048]{1,0:T(8,128)(2,1)}, u32[]{:S(2)}, u32[]{:S(2)}) collective-permute-start(bf16[256,2048]{1,0:T(8,128)(2,1)S(1)} %pad_maximum_fusion.refs_1_.refs_0_), channel_id=1, source_target_pairs={{0,48},{16,0},{32,16},{48,32},{1,49},{17,1},{33,17},{49,33},{2,50}... | collective-permute-start | bytes 3145736 | tf_op jit(solution)/shard_map/ppermute | solution.py:20
  15.9 37.0 %collective-permute-start.2 = (bf16[256,2048]{1,0:T(8,128)(2,1)S(1)}, bf16[256,2048]{1,0:T(8,128)(2,1)}, u32[]{:S(2)}, u32[]{:S(2)}) collective-permute-start(bf16[256,2048]{1,0:T(8,128)(2,1)S(1)} %pad_maximum_fusion.refs_1_.refs_0_), channel_id=1, source_target_pairs={{0,64},{64,0},{1,65},{65,1},{2,66},{66,2},{3,67},{67,3},{4,68},{68... | collective-permute-start | bytes 3145736 | tf_op jit(solution)/shard_map/ppermute | solution.py:20
  17.1 35.8 %collective-permute-start.3 = (bf16[512,512]{1,0:T(8,128)(2,1)S(1)}, bf16[512,512]{1,0:T(8,128)(2,1)S(1)}, u32[]{:S(2)}, u32[]{:S(2)}) collective-permute-start(bf16[512,512]{1,0:T(8,128)(2,1)S(1)} %copy-done.7), channel_id=1, source_target_pairs={{0,1},{1,0},{2,3},{3,2},{4,5},{5,4},{6,7},{7,6},{8,9},{9,8},{10,11... | collective-permute-start | bytes 1572872 | tf_op jit(solution)/shard_map/ppermute | solution.py:20
  54.0 201.1 %all-gather.9.cloned.1.call-start = ((), (), s32[]{:S(2)}) async-start(), calls=%async_computation.1 | async-start | bytes 13369344 | tf_op jit(solution)/shard_map/all_gather | solution.py:309
  55.2 29.8 %collective-permute-start.6 = (bf16[256,1280]{1,0:T(8,128)(2,1)S(1)}, bf16[256,1280]{1,0:T(8,128)(2,1)S(1)}, u32[]{:S(2)}, u32[]{:S(2)}) collective-permute-start(bf16[256,1280]{1,0:T(8,128)(2,1)S(1)} %slice.141), channel_id=1, source_target_pairs={{0,16},{16,32},{32,48},{48,0},{1,17},{17,33},{33,49},{49,1},{2,18}... | collective-permute-start | bytes 1966088 | tf_op jit(solution)/shard_map/ppermute | solution.py:20
  55.3 30.1 %collective-permute-start.7 = (bf16[256,1280]{1,0:T(8,128)(2,1)S(1)}, bf16[256,1280]{1,0:T(8,128)(2,1)}, u32[]{:S(2)}, u32[]{:S(2)}) collective-permute-start(bf16[256,1280]{1,0:T(8,128)(2,1)S(1)} %slice.141), channel_id=1, source_target_pairs={{0,48},{16,0},{32,16},{48,32},{1,49},{17,1},{33,17},{49,33},{2,50}... | collective-permute-start | bytes 1966088 | tf_op jit(solution)/shard_map/ppermute | solution.py:20
  59.0 23.0 %collective-permute-start.4 = (bf16[128,2048]{1,0:T(8,128)(2,1)S(1)}, bf16[128,2048]{1,0:T(8,128)(2,1)S(1)}, u32[]{:S(2)}, u32[]{:S(2)}) collective-permute-start(bf16[128,2048]{1,0:T(8,128)(2,1)S(1)} %slice.139), channel_id=1, source_target_pairs={{0,16},{16,32},{32,48},{48,0},{1,17},{17,33},{33,49},{49,1},{2,18}... | collective-permute-start | bytes 1572872 | tf_op jit(solution)/shard_map/ppermute | solution.py:20
  60.2 24.7 %collective-permute-start.5 = (bf16[128,2048]{1,0:T(8,128)(2,1)S(1)}, bf16[128,2048]{1,0:T(8,128)(2,1)S(1)}, u32[]{:S(2)}, u32[]{:S(2)}) collective-permute-start(bf16[128,2048]{1,0:T(8,128)(2,1)S(1)} %slice.140), channel_id=1, source_target_pairs={{0,48},{16,0},{32,16},{48,32},{1,49},{17,1},{33,17},{49,33},{2,50}... | collective-permute-start | bytes 1572872 | tf_op jit(solution)/shard_map/ppermute | solution.py:20
  65.2 22.6 %collective-permute-start.8 = (bf16[2,256,768]{2,1,0:T(8,128)(2,1)}, bf16[2,256,768]{2,1,0:T(8,128)(2,1)}, u32[]{:S(2)}, u32[]{:S(2)}) collective-permute-start(bf16[2,256,768]{2,1,0:T(8,128)(2,1)} %pad_maximum_fusion.2), channel_id=1, source_target_pairs={{0,64},{64,0},{1,65},{65,1},{2,66},{66,2},{3,67},{67,3},{4,68},{68... | collective-permute-start | bytes 2359304 | tf_op jit(solution)/shard_map/ppermute | solution.py:20
  82.0 9.6 %collective-permute-start.13 = (bf16[256,2048]{1,0:T(8,128)(2,1)S(1)}, bf16[256,2048]{1,0:T(8,128)(2,1)}, u32[]{:S(2)}, u32[]{:S(2)}) collective-permute-start(bf16[256,2048]{1,0:T(8,128)(2,1)S(1)} %pad_maximum_fusion.refs_1_.refs_0_), channel_id=1, source_target_pairs={{0,8},{8,0},{1,9},{9,1},{2,10},{10,2},{3,11},{11,3},{4,12},{12,4},... | collective-permute-start | bytes 3145736 | tf_op jit(solution)/shard_map/ppermute | solution.py:20
  87.8 21.1 %collective-permute-start.12 = (bf16[256,3,512]{0,2,1:T(8,128)(2,1)}, bf16[256,3,512]{0,2,1:T(8,128)(2,1)}, u32[]{:S(2)}, u32[]{:S(2)}) collective-permute-start(bf16[256,3,512]{0,2,1:T(8,128)(2,1)} %bitcast.80), channel_id=1, source_target_pairs={{1,8},{8,1},{3,10},{10,3},{5,12},{12,5},{7,14},{14,7},{17,24},{24,... | collective-permute-start | bytes 2359304 | tf_op jit(solution)/shard_map/ppermute | solution.py:24
  91.6 10.8 %collective-permute-start.9 = (bf16[128,1280]{1,0:T(8,128)(2,1)S(1)}, bf16[128,1280]{1,0:T(8,128)(2,1)S(1)}, u32[]{:S(2)}, u32[]{:S(2)}) collective-permute-start(bf16[128,1280]{1,0:T(8,128)(2,1)S(1)} %slice.144), channel_id=1, source_target_pairs={{0,16},{16,32},{32,48},{48,0},{1,17},{17,33},{33,49},{49,1},{2,18}... | collective-permute-start | bytes 983048 | tf_op jit(solution)/shard_map/ppermute | solution.py:20
  91.7 10.7 %collective-permute-start.10 = (bf16[128,1280]{1,0:T(8,128)(2,1)S(1)}, bf16[128,1280]{1,0:T(8,128)(2,1)S(1)}, u32[]{:S(2)}, u32[]{:S(2)}) collective-permute-start(bf16[128,1280]{1,0:T(8,128)(2,1)S(1)} %slice.145), channel_id=1, source_target_pairs={{0,48},{16,0},{32,16},{48,32},{1,49},{17,1},{33,17},{49,33},{2,50}... | collective-permute-start | bytes 983048 | tf_op jit(solution)/shard_map/ppermute | solution.py:20
  94.4 14.4 %collective-permute-start.11 = (bf16[2,128,768]{2,1,0:T(8,128)(2,1)S(1)}, bf16[2,128,768]{2,1,0:T(8,128)(2,1)S(1)}, u32[]{:S(2)}, u32[]{:S(2)}) collective-permute-start(bf16[2,128,768]{2,1,0:T(8,128)(2,1)S(1)} %pad_maximum_fusion.4), channel_id=1, source_target_pairs={{0,64},{64,0},{1,65},{65,1},{2,66},{66,2},{3,67},{67,3},{4,68},{68... | collective-permute-start | bytes 1179656 | tf_op jit(solution)/shard_map/ppermute | solution.py:20
  94.8 16.8 %collective-permute-start.21 = (bf16[2,256,768]{2,1,0:T(8,128)(2,1)}, bf16[2,256,768]{2,1,0:T(8,128)(2,1)}, u32[]{:S(2)}, u32[]{:S(2)}) collective-permute-start(bf16[2,256,768]{2,1,0:T(8,128)(2,1)} %collective-permute-done.8.refs_9_.refs_8_), channel_id=1, source_target_pairs={{0,8},{8,0},{1,9},{9,1},{2,10},{10,2},{3,11},{11,3},{4,12},{12,4},... | collective-permute-start | bytes 2359304 | tf_op jit(solution)/shard_map/ppermute | solution.py:20
  114.0 175.9 %all-gather.11.cloned.1.call-start = ((), (), s32[]{:S(2)}) async-start(), calls=%async_computation.2 | async-start | bytes 4456448 | tf_op jit(solution)/shard_map/all_gather | solution.py:309
  114.1 9.5 %collective-permute-start.55 = (bf16[512,256]{1,0:T(8,128)(2,1)S(1)}, bf16[512,256]{1,0:T(8,128)(2,1)S(1)}, u32[]{:S(2)}, u32[]{:S(2)}) collective-permute-start(bf16[512,256]{1,0:T(8,128)(2,1)S(1)} %slice_bitcast_fusion.10), channel_id=1, source_target_pairs={{1,8},{8,1},{3,10},{10,3},{5,12},{12,5},{7,14},{14,7},{17,24},{24,... | collective-permute-start | bytes 786440 | tf_op jit(solution)/shard_map/ppermute | solution.py:24
  149.3 20.2 %collective-permute-start.32 = (bf16[256,1024]{1,0:T(8,128)(2,1)}, bf16[256,1024]{1,0:T(8,128)(2,1)}, u32[]{:S(2)}, u32[]{:S(2)}) collective-permute-start(bf16[256,1024]{1,0:T(8,128)(2,1)} %get-tuple-element.97), channel_id=1, source_target_pairs={{0,4},{2,6},{4,0},{6,2},{1,5},{3,7},{5,1},{7,3},{8,12},{10,14},{12... | collective-permute-start | bytes 1572872 | tf_op jit(solution)/shard_map/ppermute | solution.py:20
  152.9 24.2 %collective-permute-start.31 = (bf16[256,1024]{1,0:T(8,128)(2,1)}, bf16[256,1024]{1,0:T(8,128)(2,1)}, u32[]{:S(2)}, u32[]{:S(2)}) collective-permute-start(bf16[256,1024]{1,0:T(8,128)(2,1)} %get-tuple-element.96), channel_id=1, source_target_pairs={{0,6},{2,0},{4,2},{6,4},{1,7},{3,1},{5,3},{7,5},{8,14},{10,8},{12,... | collective-permute-start | bytes 1572872 | tf_op jit(solution)/shard_map/ppermute | solution.py:20
  153.3 24.7 %collective-permute-start.30 = (bf16[256,1024]{1,0:T(8,128)(2,1)}, bf16[256,1024]{1,0:T(8,128)(2,1)}, u32[]{:S(2)}, u32[]{:S(2)}) collective-permute-start(bf16[256,1024]{1,0:T(8,128)(2,1)} %get-tuple-element.95), channel_id=1, source_target_pairs={{0,2},{2,4},{4,6},{6,0},{1,3},{3,5},{5,7},{7,1},{8,10},{10,12},{12... | collective-permute-start | bytes 1572872 | tf_op jit(solution)/shard_map/ppermute | solution.py:20
  158.9 27.7 %collective-permute-start.25 = (bf16[512,512]{1,0:T(8,128)(2,1)}, bf16[512,512]{1,0:T(8,128)(2,1)S(1)}, u32[]{:S(2)}, u32[]{:S(2)}) collective-permute-start(bf16[512,512]{1,0:T(8,128)(2,1)} %param.8), channel_id=1, source_target_pairs={{1,8},{8,1},{3,10},{10,3},{5,12},{12,5},{7,14},{14,7},{17,24},{24,... | collective-permute-start | bytes 1572872 | tf_op jit(solution)/shard_map/ppermute | solution.py:24
  168.6 19.6 %collective-permute-start.27 = (bf16[256,1024]{1,0:T(8,128)(2,1)S(1)}, bf16[256,1024]{1,0:T(8,128)(2,1)S(1)}, u32[]{:S(2)}, u32[]{:S(2)}) collective-permute-start(bf16[256,1024]{1,0:T(8,128)(2,1)S(1)} %get-tuple-element.90), channel_id=1, source_target_pairs={{0,2},{2,4},{4,6},{6,0},{1,3},{3,5},{5,7},{7,1},{8,10},{10,12},{12... | collective-permute-start | bytes 1572872 | tf_op jit(solution)/shard_map/ppermute | solution.py:20
  169.4 24.0 %collective-permute-start.28 = (bf16[256,1024]{1,0:T(8,128)(2,1)S(1)}, bf16[256,1024]{1,0:T(8,128)(2,1)S(1)}, u32[]{:S(2)}, u32[]{:S(2)}) collective-permute-start(bf16[256,1024]{1,0:T(8,128)(2,1)S(1)} %get-tuple-element.91), channel_id=1, source_target_pairs={{0,6},{2,0},{4,2},{6,4},{1,7},{3,1},{5,3},{7,5},{8,14},{10,8},{12,... | collective-permute-start | bytes 1572872 | tf_op jit(solution)/shard_map/ppermute | solution.py:20
  177.2 21.9 %collective-permute-start.29 = (bf16[256,1024]{1,0:T(8,128)(2,1)S(1)}, bf16[256,1024]{1,0:T(8,128)(2,1)S(1)}, u32[]{:S(2)}, u32[]{:S(2)}) collective-permute-start(bf16[256,1024]{1,0:T(8,128)(2,1)S(1)} %get-tuple-element.92), channel_id=1, source_target_pairs={{0,4},{2,6},{4,0},{6,2},{1,5},{3,7},{5,1},{7,3},{8,12},{10,14},{12... | collective-permute-start | bytes 1572872 | tf_op jit(solution)/shard_map/ppermute | solution.py:20
  179.8 24.1 %collective-permute-start.34 = (bf16[256,512]{1,0:T(8,128)(2,1)S(1)}, bf16[256,512]{1,0:T(8,128)(2,1)S(1)}, u32[]{:S(2)}, u32[]{:S(2)}) collective-permute-start(bf16[256,512]{1,0:T(8,128)(2,1)S(1)} %get-tuple-element.137), channel_id=1, source_target_pairs={{1,8},{8,1},{3,10},{10,3},{5,12},{12,5},{7,14},{14,7},{17,24},{24,... | collective-permute-start | bytes 786440 | tf_op jit(solution)/shard_map/ppermute | solution.py:391
  186.6 17.3 %collective-permute-start.35 = (bf16[256,512]{1,0:T(8,128)(2,1)S(1)}, bf16[256,512]{1,0:T(8,128)(2,1)S(1)}, u32[]{:S(2)}, u32[]{:S(2)}) collective-permute-start(bf16[256,512]{1,0:T(8,128)(2,1)S(1)} %get-tuple-element.137), channel_id=1, source_target_pairs={{0,8},{9,1},{2,10},{11,3},{4,12},{13,5},{6,14},{15,7},{16,24},{25,... | collective-permute-start | bytes 786440 | tf_op jit(solution)/shard_map/ppermute | solution.py:392
  188.2 15.7 %collective-permute-start.33 = (bf16[256,512]{1,0:T(8,128)(2,1)S(1)}, bf16[256,512]{1,0:T(8,128)(2,1)S(1)}, u32[]{:S(2)}, u32[]{:S(2)}) collective-permute-start(bf16[256,512]{1,0:T(8,128)(2,1)S(1)} %get-tuple-element.138), channel_id=1, source_target_pairs={{1,0},{8,9},{3,2},{10,11},{5,4},{12,13},{7,6},{14,15},{17,16},{24,... | collective-permute-start | bytes 786440 | tf_op jit(solution)/shard_map/ppermute | solution.py:390
  204.4 25.2 %collective-permute-start.37 = (bf16[256,512]{1,0:T(8,128)(2,1)S(1)}, bf16[256,512]{1,0:T(8,128)(2,1)S(1)}, u32[]{:S(2)}, u32[]{:S(2)}) collective-permute-start(bf16[256,512]{1,0:T(8,128)(2,1)S(1)} %get-tuple-element.135), channel_id=1, source_target_pairs={{1,8},{8,1},{3,10},{10,3},{5,12},{12,5},{7,14},{14,7},{17,24},{24,... | collective-permute-start | bytes 786440 | tf_op jit(solution)/shard_map/ppermute | solution.py:391
  208.3 21.2 %collective-permute-start.36 = (bf16[256,512]{1,0:T(8,128)(2,1)S(1)}, bf16[256,512]{1,0:T(8,128)(2,1)S(1)}, u32[]{:S(2)}, u32[]{:S(2)}) collective-permute-start(bf16[256,512]{1,0:T(8,128)(2,1)S(1)} %get-tuple-element.136), channel_id=1, source_target_pairs={{1,0},{8,9},{3,2},{10,11},{5,4},{12,13},{7,6},{14,15},{17,16},{24,... | collective-permute-start | bytes 786440 | tf_op jit(solution)/shard_map/ppermute | solution.py:390
  213.8 15.7 %collective-permute-start.39 = (bf16[256,512]{1,0:T(8,128)(2,1)S(1)}, bf16[256,512]{1,0:T(8,128)(2,1)S(1)}, u32[]{:S(2)}, u32[]{:S(2)}) collective-permute-start(bf16[256,512]{1,0:T(8,128)(2,1)S(1)} %add_convert_fusion.5.refs_8_), channel_id=1, source_target_pairs={{0,2},{2,4},{4,6},{6,0},{1,3},{3,5},{5,7},{7,1},{8,10},{10,12},{12... | collective-permute-start | bytes 786440 | tf_op jit(solution)/shard_map/ppermute | solution.py:20
  215.5 14.1 %collective-permute-start.40 = (bf16[256,512]{1,0:T(8,128)(2,1)S(1)}, bf16[256,512]{1,0:T(8,128)(2,1)S(1)}, u32[]{:S(2)}, u32[]{:S(2)}) collective-permute-start(bf16[256,512]{1,0:T(8,128)(2,1)S(1)} %add_convert_fusion.5.refs_8_), channel_id=1, source_target_pairs={{0,6},{2,0},{4,2},{6,4},{1,7},{3,1},{5,3},{7,5},{8,14},{10,8},{12,... | collective-permute-start | bytes 786440 | tf_op jit(solution)/shard_map/ppermute | solution.py:20
  216.6 19.7 %collective-permute-start.41 = (bf16[256,512]{1,0:T(8,128)(2,1)S(1)}, bf16[256,512]{1,0:T(8,128)(2,1)S(1)}, u32[]{:S(2)}, u32[]{:S(2)}) collective-permute-start(bf16[256,512]{1,0:T(8,128)(2,1)S(1)} %add_convert_fusion.5.refs_8_), channel_id=1, source_target_pairs={{0,4},{2,6},{4,0},{6,2},{1,5},{3,7},{5,1},{7,3},{8,12},{10,14},{12... | collective-permute-start | bytes 786440 | tf_op jit(solution)/shard_map/ppermute | solution.py:20
  229.5 9.7 %collective-permute-start.49 = (bf16[256,512]{1,0:T(8,128)(2,1)S(1)}, bf16[256,512]{1,0:T(8,128)(2,1)S(1)}, u32[]{:S(2)}, u32[]{:S(2)}) collective-permute-start(bf16[256,512]{1,0:T(8,128)(2,1)S(1)} %add_convert_fusion.5.refs_8_), channel_id=1, source_target_pairs={{0,8},{8,0},{1,9},{9,1},{2,10},{10,2},{3,11},{11,3},{4,12},{12,4},... | collective-permute-start | bytes 786440 | tf_op jit(solution)/shard_map/ppermute | solution.py:20
  236.4 14.1 %collective-permute-start.42 = (bf16[256,512]{1,0:T(8,128)(2,1)S(1)}, bf16[256,512]{1,0:T(8,128)(2,1)S(1)}, u32[]{:S(2)}, u32[]{:S(2)}) collective-permute-start(bf16[256,512]{1,0:T(8,128)(2,1)S(1)} %add_convert_fusion.4.refs_0_), channel_id=1, source_target_pairs={{0,2},{2,4},{4,6},{6,0},{1,3},{3,5},{5,7},{7,1},{8,10},{10,12},{12... | collective-permute-start | bytes 786440 | tf_op jit(solution)/shard_map/ppermute | solution.py:20
  236.9 13.7 %collective-permute-start.43 = (bf16[256,512]{1,0:T(8,128)(2,1)S(1)}, bf16[256,512]{1,0:T(8,128)(2,1)S(1)}, u32[]{:S(2)}, u32[]{:S(2)}) collective-permute-start(bf16[256,512]{1,0:T(8,128)(2,1)S(1)} %add_convert_fusion.4.refs_0_), channel_id=1, source_target_pairs={{0,6},{2,0},{4,2},{6,4},{1,7},{3,1},{5,3},{7,5},{8,14},{10,8},{12,... | collective-permute-start | bytes 786440 | tf_op jit(solution)/shard_map/ppermute | solution.py:20
  239.2 11.9 %collective-permute-start.44 = (bf16[256,512]{1,0:T(8,128)(2,1)S(1)}, bf16[256,512]{1,0:T(8,128)(2,1)S(1)}, u32[]{:S(2)}, u32[]{:S(2)}) collective-permute-start(bf16[256,512]{1,0:T(8,128)(2,1)S(1)} %add_convert_fusion.4.refs_0_), channel_id=1, source_target_pairs={{0,4},{2,6},{4,0},{6,2},{1,5},{3,7},{5,1},{7,3},{8,12},{10,14},{12... | collective-permute-start | bytes 786440 | tf_op jit(solution)/shard_map/ppermute | solution.py:20
  239.2 12.0 %collective-permute-start.45 = (bf16[256,512]{1,0:T(8,128)(2,1)S(1)}, bf16[256,512]{1,0:T(8,128)(2,1)S(1)}, u32[]{:S(2)}, u32[]{:S(2)}) collective-permute-start(bf16[256,512]{1,0:T(8,128)(2,1)S(1)} %add_convert_fusion.4.refs_0_), channel_id=1, source_target_pairs={{0,8},{8,0},{1,9},{9,1},{2,10},{10,2},{3,11},{11,3},{4,12},{12,4},... | collective-permute-start | bytes 786440 | tf_op jit(solution)/shard_map/ppermute | solution.py:20
  239.2 12.4 %collective-permute-start.50 = (bf16[256,512]{1,0:T(8,128)(2,1)S(1)}, bf16[256,512]{1,0:T(8,128)(2,1)S(1)}, u32[]{:S(2)}, u32[]{:S(2)}) collective-permute-start(bf16[256,512]{1,0:T(8,128)(2,1)S(1)} %collective-permute-done.39.refs_9_), channel_id=1, source_target_pairs={{0,8},{8,0},{1,9},{9,1},{2,10},{10,2},{3,11},{11,3},{4,12},{12,4},... | collective-permute-start | bytes 786440 | tf_op jit(solution)/shard_map/ppermute | solution.py:20
  252.4 18.9 %collective-permute-start.53 = (f32[138,512]{1,0:T(8,128)S(1)}, f32[138,512]{1,0:T(8,128)}, u32[]{:S(2)}, u32[]{:S(2)}) collective-permute-start(f32[138,512]{1,0:T(8,128)S(1)} %copy-done.9), channel_id=1, source_target_pairs={{1,8},{8,1},{3,10},{10,3},{5,12},{12,5},{7,14},{14,7},{17,24},{24,... | collective-permute-start | bytes 847880 | tf_op jit(solution)/shard_map/ppermute | solution.py:24
  269.8 12.5 %collective-permute-start.54 = (bf16[160,1024]{1,0:T(8,128)(2,1)}, bf16[160,1024]{1,0:T(8,128)(2,1)S(1)}, u32[]{:S(2)}, u32[]{:S(2)}) collective-permute-start(bf16[160,1024]{1,0:T(8,128)(2,1)} %get-tuple-element.115), channel_id=1, source_target_pairs={{0,1},{1,16},{16,17},{17,32},{32,33},{33,48},{48,49},{49,64},{64,6... | collective-permute-start | bytes 983048 | tf_op jit(solution)/shard_map/ppermute | solution.py:30
  301.3 14.6 %collective-permute-start.63 = (bf16[256,512]{1,0:T(8,128)(2,1)S(1)}, bf16[256,512]{1,0:T(8,128)(2,1)S(1)}, u32[]{:S(2)}, u32[]{:S(2)}) collective-permute-start(bf16[256,512]{1,0:T(8,128)(2,1)S(1)} %get-tuple-element.134), channel_id=1, source_target_pairs={{0,6},{2,0},{4,2},{6,4},{1,7},{3,1},{5,3},{7,5},{8,14},{10,8},{12,... | collective-permute-start | bytes 786440 | tf_op jit(solution)/shard_map/ppermute | solution.py:20
  303.8 13.6 %collective-permute-start.62 = (bf16[256,512]{1,0:T(8,128)(2,1)S(1)}, bf16[256,512]{1,0:T(8,128)(2,1)S(1)}, u32[]{:S(2)}, u32[]{:S(2)}) collective-permute-start(bf16[256,512]{1,0:T(8,128)(2,1)S(1)} %get-tuple-element.132), channel_id=1, source_target_pairs={{0,2},{2,4},{4,6},{6,0},{1,3},{3,5},{5,7},{7,1},{8,10},{10,12},{12... | collective-permute-start | bytes 786440 | tf_op jit(solution)/shard_map/ppermute | solution.py:20
  304.7 17.1 %collective-permute-start.59 = (bf16[256,512]{1,0:T(8,128)(2,1)S(1)}, bf16[256,512]{1,0:T(8,128)(2,1)S(1)}, u32[]{:S(2)}, u32[]{:S(2)}) collective-permute-start(bf16[256,512]{1,0:T(8,128)(2,1)S(1)} %get-tuple-element.130), channel_id=1, source_target_pairs={{0,4},{2,6},{4,0},{6,2},{1,5},{3,7},{5,1},{7,3},{8,12},{10,14},{12... | collective-permute-start | bytes 786440 | tf_op jit(solution)/shard_map/ppermute | solution.py:20
  306.6 20.6 %collective-permute-start.58 = (bf16[256,512]{1,0:T(8,128)(2,1)S(1)}, bf16[256,512]{1,0:T(8,128)(2,1)S(1)}, u32[]{:S(2)}, u32[]{:S(2)}) collective-permute-start(bf16[256,512]{1,0:T(8,128)(2,1)S(1)} %get-tuple-element.131), channel_id=1, source_target_pairs={{0,6},{2,0},{4,2},{6,4},{1,7},{3,1},{5,3},{7,5},{8,14},{10,8},{12,... | collective-permute-start | bytes 786440 | tf_op jit(solution)/shard_map/ppermute | solution.py:20
  310.3 17.6 %collective-permute-start.57 = (bf16[256,512]{1,0:T(8,128)(2,1)S(1)}, bf16[256,512]{1,0:T(8,128)(2,1)S(1)}, u32[]{:S(2)}, u32[]{:S(2)}) collective-permute-start(bf16[256,512]{1,0:T(8,128)(2,1)S(1)} %get-tuple-element.129), channel_id=1, source_target_pairs={{0,2},{2,4},{4,6},{6,0},{1,3},{3,5},{5,7},{7,1},{8,10},{10,12},{12... | collective-permute-start | bytes 786440 | tf_op jit(solution)/shard_map/ppermute | solution.py:20
  317.6 14.6 %collective-permute-start.65 = (bf16[256,512]{1,0:T(8,128)(2,1)S(1)}, bf16[256,512]{1,0:T(8,128)(2,1)S(1)}, u32[]{:S(2)}, u32[]{:S(2)}) collective-permute-start(bf16[256,512]{1,0:T(8,128)(2,1)S(1)} %fusion.3), channel_id=1, source_target_pairs={{1,8},{8,1},{3,10},{10,3},{5,12},{12,5},{7,14},{14,7},{17,24},{24,... | collective-permute-start | bytes 786440 | tf_op jit(solution)/shard_map/ppermute | solution.py:24
  (36 other events, 414.3 us)
Sparse Core Ops, SparseCore 0:
  54.1 48.6 all-gather.6
  114.2 106.2 all-gather.8
  222.6 57.8 all-gather.10
